TPU v7x, 256 devices: a whole 4x4x8 slice. The times are simulated.
256 devices in a mesh: dp: 64 (over y, z, x_lo), width: 4 (over x_hi, core).
Axes of the slice: x: 4 (x_hi: 2, x_lo: 2; x = x_hi * 2 + x_lo), y: 4, z: 8, core: 2. Of those that a mesh axis runs over, the one named last changes fastest.
Arguments:
- queries: bfloat16 [5632, 4096], P('dp', 'width'), may hold values from -12 to 12
- passages: bfloat16 [5632, 4096], P('dp', 'width'), may hold values from -12 to 12
- negatives: bfloat16 [5632, 4096], P('dp', 'width'), may hold values from -6 to 6
- neg_owner: int32 [5632, 7], P('dp'), may hold values from 0 to 63, all different within a row; in each aligned block of 88 rows (0 to 87, 88 to 175, ...) at most 19 rows name the same one
- neg_row: int32 [5632, 7], P('dp'), may hold values from 0 to 87
Outputs:
- row_loss: float32 [5632], P('dp')
- grad_queries: bfloat16 [5632, 4096], P('dp', 'width')
- grad_passages: bfloat16 [5632, 4096], P('dp', 'width')
- grad_negatives: bfloat16 [5632, 4096], P('dp', 'width')
Inputs may be any that keep to these rules, and one draw needn't show every extreme that they name: `neg_owner`: the 7 owners of one query differ. Among the queries of one device, no owner is named more than 19 times, a bound that some block reaches.
All inputs are finite; a program needn't handle non-finite values.
Results may differ from a plain program's by a relative error of at most 0.0049.
Values may be sent and summed in bfloat16 or wider, within the bound.
No kernel may reach another device: no remote copies, remote signals or barrier semaphores. Data moves between devices by JAX's collectives and lax.ppermute only.
A program may use at most 128 MiB of HBM per device.

v0:
```python
import jax
import jax.numpy as jnp
from jax import lax
from jax.sharding import PartitionSpec as P


def local(queries, passages, negatives, neg_owner, neg_row):
    dev_count = lax.axis_size("dp")
    width_count = lax.axis_size("width")
    row_count = queries.shape[0]
    feature_count = queries.shape[1]
    neg_count = neg_owner.shape[1]
    all_rows = row_count * dev_count
    score_scale = (feature_count * width_count) ** (-0.5)
    capacity = max(2, min(row_count, 2 * row_count * neg_count // dev_count))
    my_block = lax.axis_index("dp")
    ref_count = row_count * neg_count
    owner_flat = neg_owner.reshape(ref_count)
    row_flat = neg_row.reshape(ref_count)
    owner_hits = (owner_flat[:, None] == jnp.arange(dev_count, dtype=jnp.int32)[None, :]).astype(
        jnp.int32
    )
    earlier = jnp.cumsum(owner_hits, axis=0) - owner_hits
    slot_index = jnp.sum(earlier * owner_hits, axis=1)
    requests = (
        jnp.full((dev_count, capacity), row_count, jnp.int32)
        .at[owner_flat, slot_index]
        .set(row_flat)
    )
    asked_rows = lax.all_to_all(requests, "dp", split_axis=0, concat_axis=0, tiled=True)
    found_rows = jnp.take(negatives, jnp.minimum(asked_rows, row_count - 1), axis=0)
    asked_rows, fetched = (
        asked_rows,
        lax.all_to_all(found_rows, "dp", split_axis=0, concat_axis=0, tiled=True),
    )
    picked_rows = fetched[owner_flat, slot_index].reshape(row_count, neg_count, feature_count)
    every_passage = lax.all_gather(passages, "dp", axis=0, tiled=True)
    part_scores = jnp.einsum(
        "qd,pd->qp", queries, every_passage, preferred_element_type=jnp.float32
    )
    part_neg = jnp.einsum("qd,qkd->qk", queries, picked_rows, preferred_element_type=jnp.float32)
    target_ids = my_block * row_count + jnp.arange(row_count, dtype=jnp.int32)[:, None]
    scores, neg_scores = lax.psum((part_scores, part_neg), "width")
    scores = scores * score_scale
    neg_scores = neg_scores * score_scale
    row_peak = jnp.maximum(jnp.max(scores, axis=1), jnp.max(neg_scores, axis=1))
    row_total = jnp.sum(jnp.exp(scores - row_peak[:, None]), axis=1) + jnp.sum(
        jnp.exp(neg_scores - row_peak[:, None]), axis=1
    )
    log_total = row_peak + jnp.log(row_total)
    column_hits = jnp.arange(all_rows, dtype=jnp.int32)[None, :] == target_ids
    positive = jnp.sum(jnp.where(column_hits, scores, 0.0), axis=1)
    soft_weight = (jnp.exp(scores - log_total[:, None]) - column_hits.astype(jnp.float32)).astype(
        jnp.bfloat16
    )
    row_loss = log_total - positive
    neg_weight = jnp.exp(neg_scores - log_total[:, None])
    neg_term = jnp.sum(neg_weight[:, :, None] * picked_rows.astype(jnp.float32), axis=1)
    grad_queries = (
        score_scale
        * (jnp.dot(soft_weight, every_passage, preferred_element_type=jnp.float32) + neg_term)
    ).astype(jnp.bfloat16)
    block_weights = lax.all_to_all(soft_weight, "dp", split_axis=1, concat_axis=0, tiled=True)
    grad_sum = lax.dot_general(
        block_weights,
        lax.all_gather(queries, "dp", axis=0, tiled=True),
        (((0,), (0,)), ((), ())),
        preferred_element_type=jnp.float32,
    )
    grad_passages = (score_scale * grad_sum).astype(jnp.bfloat16)
    contribution = (
        (score_scale * neg_weight)[:, :, None] * queries.astype(jnp.float32)[:, None, :]
    ).astype(jnp.bfloat16)
    outgoing = (
        jnp.zeros((dev_count, capacity, feature_count), jnp.bfloat16)
        .at[owner_flat, slot_index]
        .set(contribution.reshape(ref_count, feature_count))
    )
    returned = lax.all_to_all(outgoing, "dp", split_axis=0, concat_axis=0, tiled=True)
    grad_pool = jax.ops.segment_sum(
        returned.reshape(dev_count * capacity, feature_count).astype(jnp.float32),
        asked_rows.reshape(dev_count * capacity),
        num_segments=row_count,
    )
    return (row_loss, grad_queries, grad_passages, grad_pool.astype(jnp.bfloat16))


def solution(mesh):
    in_specs = (P("dp", "width"), P("dp", "width"), P("dp", "width"), P("dp", None), P("dp", None))
    out_specs = (P("dp"), P("dp", "width"), P("dp", "width"), P("dp", "width"))
    return jax.shard_map(local, mesh=mesh, in_specs=in_specs, out_specs=out_specs, check_vma=False)
```

profile of v0, /device:TPU:0, one launch (start us, length us, event | category | flops | bytes accessed | tf_op | source)
XLA Modules:
  0.0 820.3 jit_solution(4545293239464752979)
XLA Ops:
  7.2 0.0 all-gather.3.cloned.1.call-start
  7.2 0.7 all-gather.3.cloned.1.call-update
  7.9 0.0 all-reduce.3.cloned.1.call-start
  8.0 326.7 %all-gather.3.cloned.1.call-done = bf16[5632,1024]{1,0:T(8,128)(2,1)} async-done(((bf16[88,1024]{1,0:T(8,128)(2,1)}), bf16[5632,1024]{1,0:T(8,128)(2,1)}) %all-gather.3.cloned.1.call-update) | async-done | bytes 11534352 | tf_op jit(solution)/shard_map/all_gather | solution.py:37
  334.6 9.3 %fusion.13 = f32[88,5632]{1,0:T(8,128)} fusion(bf16[88,1024]{1,0:T(8,128)(2,1)} %param.5, bf16[5632,1024]{1,0:T(8,128)(2,1)} %all-gather.3.cloned.1.call-done), kind=kOutput, calls=%fused_computation.51 | convolution fusion | flops 1015021568 | bytes 13697024 | tf_op jit(solution)/shard_map/qd,pd->qp/dot_general | solution.py:38
  343.9 0.0 all-reduce.3.cloned.1.call-update
  343.9 0.0 all-gather.5.cloned.1.call-start
  344.0 0.7 all-gather.5.cloned.1.call-update
  344.7 0.1 copy.20
  344.8 0.2 eq.35
  345.0 0.2 reshape.136
  345.2 1.5 reduce-window.6
  346.7 0.3 slice_reduce_fusion
  347.0 0.1 copy.24
  347.1 0.2 reshape.159
  347.2 0.1 bitcast_bitcast_fusion
  347.5 32.8 %scatter_fusion = s32[64,19]{0,1:T(8,128)S(1)} fusion(s32[64,19]{0,1:T(8,128)S(1)} %broadcast_in_dim.22, s32[616]{0:T(1024)S(1)} %get-tuple-element.7, s32[616]{0:T(1024)S(1)} %reshape.159), kind=kCustom, calls=%fused_computation.2 | custom fusion | bytes 12320 | tf_op jit(solution)/shard_map/scatter | solution.py:28
  380.3 0.1 copy.25
  380.3 17.6 %all_to_all.38 = s32[64,1,19]{2,1,0:T(1,128)S(1)} all-to-all(s32[64,1,19]{2,1,0:T(1,128)S(1)} %copy.25), channel_id=1, replica_groups=mesh['dp'=64,'width'=4] {'dp'}, dimensions={0} | all-to-all | bytes 9728 | tf_op jit(solution)/shard_map/all_to_all | solution.py:30
  398.0 0.1 copy.26
  398.1 0.1 copy.28
  398.1 0.1 reshape.145
  398.3 4.4 gather_fusion
  402.7 2.5 reshape.144
  405.3 0.1 copy.27
  405.4 3.3 broadcast_select_fusion
  408.6 5.8 all-to-all-start.1
  414.4 53.3 %all-to-all-done.1 = bf16[64,19,1024]{2,1,0:T(8,128)(2,1)} async-done(((bf16[64,19,1024]{2,1,0:T(8,128)(2,1)}), bf16[64,19,1024]{2,1,0:T(8,128)(2,1)}, u32[]{:S(2)}, u32[]{:S(2)}) %all-to-all-start.1) | async-done | bytes 2490400 | tf_op jit(solution)/shard_map/all_to_all | solution.py:34
  467.8 3.3 copy.29
  471.1 11.8 %gather_fusion.1 = bf16[616,1024]{1,0:T(8,128)(2,1)} fusion(bf16[64,19,1024]{2,0,1:T(8,128)(2,1)S(1)} %copy.29, s32[616]{0:T(1024)S(1)} %get-tuple-element.6), kind=kCustom, calls=%fused_computation.1 | custom fusion | bytes 2528064 | tf_op jit(solution)/shard_map/gather | solution.py:36
  482.9 2.3 reshape.140
  485.2 0.9 fusion.3
  486.1 15.6 %psum.15 = f32[88,7]{1,0:T(8,128)S(1)} all-reduce(f32[88,7]{1,0:T(8,128)S(1)} %bitcast.38), channel_id=1, replica_groups=mesh['dp'=64,'width'=4] {'width'}, use_global_device_ids=true, to_apply=%region_6.7 | all-reduce | flops 616 | bytes 4928 | tf_op jit(solution)/shard_map/psum | solution.py:43
  501.8 0.1 multiply_reduce_fusion.2
  501.9 0.0 all-reduce.3.cloned.1.call-done
  501.9 1.9 multiply_reduce_fusion.1
  503.9 0.2 exponential_reduce_fusion.1
  504.1 0.0 copy-done.2
  504.1 0.8 select_reduce_fusion
  504.8 0.5 fusion.12
  505.4 0.6 subtract_convert_fusion
  505.9 1.5 copy.35
  507.5 8.3 %all-to-all-start.2 = ((bf16[88,64,88]{0,2,1:T(8,128)(2,1)}), bf16[88,64,88]{0,2,1:T(8,128)(2,1)}, u32[]{:S(2)}, u32[]{:S(2)}) async-start(bf16[88,64,88]{0,2,1:T(8,128)(2,1)} %bitcast.7), calls=%async_computation.2 | async-start | bytes 2883584 | tf_op jit(solution)/shard_map/all_to_all | solution.py:63
  515.8 0.3 mul.62
  516.2 1.9 mul.63
  518.1 0.1 broadcast_multiply_fusion
  518.1 0.2 mul.60
  518.3 3.0 multiply_convert_fusion
  521.3 0.3 broadcast_in_dim.47
  521.6 62.1 %scatter_fusion.1 = bf16[64,19,1024]{2,0,1:T(8,128)(2,1)S(1)} fusion(bf16[64,19,1024]{2,0,1:T(8,128)(2,1)S(1)} %broadcast_in_dim.47, s32[616]{0:T(1024)S(1)} %get-tuple-element.7, bf16[616,1024]{1,0:T(8,128)(2,1)} %multiply_convert_fusion), kind=kCustom, calls=%fused_computation.3 | custom fusion | bytes 3789632 | tf_op jit(solution)/shard_map/scatter | solution.py:77
  583.8 3.0 copy.32
  586.8 11.3 %all-to-all-start.3 = ((bf16[64,19,1024]{2,1,0:T(8,128)(2,1)}), bf16[64,19,1024]{2,1,0:T(8,128)(2,1)}, u32[]{:S(2)}, u32[]{:S(2)}) async-start(bf16[64,19,1024]{2,1,0:T(8,128)(2,1)} %copy.32), calls=%async_computation.3 | async-start | bytes 6291456 | tf_op jit(solution)/shard_map/all_to_all | solution.py:79
  598.2 0.5 broadcast.198
  598.7 0.7 reduce.8
  599.4 0.1 reshape.171
  599.6 1.0 multiply_reduce_fusion
  600.6 7.0 fusion.1
  607.6 1.7 copy.31
  609.3 3.1 all_to_all.32
  612.4 173.8 %all-gather.5.cloned.1.call-done = bf16[5632,1024]{1,0:T(8,128)(2,1)} async-done(((bf16[88,1024]{1,0:T(8,128)(2,1)}), bf16[5632,1024]{1,0:T(8,128)(2,1)}) %all-gather.5.cloned.1.call-update) | async-done | bytes 11534352 | tf_op jit(solution)/shard_map/all_gather | solution.py:66
  786.2 6.9 fusion.2
  793.1 4.9 reshape.173
  798.0 15.0 %scatter_custom_fusion.2 = f32[88,1024]{1,0:T(8,128)S(1)} fusion(s32[1216]{0:T(1024)S(1)} %reshape.171, f32[1216,1024]{1,0:T(8,128)} %reshape.173, f32[]{:T(128)} %constant.22.clone.1), kind=kCustom, calls=%fused_computation.20 | custom fusion | flops 1245184 | bytes 360960 | tf_op jit(solution)/shard_map/scatter-add | solution.py:80
  813.0 0.7 convert_element_type.45
  (32 shorter events, 0.2 us)
Async XLA Ops:
  7.2 391.1 %copy-start = (bf16[88,1024]{1,0:T(8,128)(2,1)S(1)}, bf16[88,1024]{1,0:T(8,128)(2,1)}, u32[]{:S(2)}) copy-start(bf16[88,1024]{1,0:T(8,128)(2,1)} %param.7) | copy-start | bytes 540676
  7.2 327.4 %all-gather.3.cloned.1.call-start = ((), (), s32[]{:S(2)}) async-start(), calls=%async_computation.4 | async-start | bytes 11714560 | tf_op jit(solution)/shard_map/all_gather | solution.py:37
  7.9 494.0 %all-reduce.3.cloned.1.call-start = ((), (), s32[]{:S(2)}) async-start(), calls=%async_computation.5 | async-start | bytes 3964928 | tf_op jit(solution)/shard_map/psum | solution.py:43
  343.9 0.8 copy-start.8
  343.9 3.1 copy-start.9
  343.9 442.2 %all-gather.5.cloned.1.call-start = ((), (), s32[]{:S(2)}) async-start(), calls=%async_computation.6 | async-start | bytes 11714560 | tf_op jit(solution)/shard_map/all_gather | solution.py:66
  408.6 59.1 %all-to-all-start.1 = ((bf16[64,19,1024]{2,1,0:T(8,128)(2,1)}), bf16[64,19,1024]{2,1,0:T(8,128)(2,1)}, u32[]{:S(2)}, u32[]{:S(2)}) async-start(bf16[64,19,1024]{2,1,0:T(8,128)(2,1)} %broadcast_select_fusion), calls=%async_computation.1 | async-start | bytes 6291456 | tf_op jit(solution)/shard_map/all_to_all | solution.py:34
  482.9 2.3 copy-start.7
  485.2 18.7 %copy-start.5 = (bf16[88,7,1024]{2,1,0:T(8,128)(2,1)}, bf16[88,7,1024]{2,1,0:T(8,128)(2,1)S(1)}, u32[]{:S(2)}) copy-start(bf16[88,7,1024]{2,1,0:T(8,128)(2,1)S(1)} %reshape.140) | copy-start | bytes 3784708
  501.9 2.2 copy-start.2
  505.9 1.5 copy-start.3
  507.5 79.4 %all-to-all-start.2 = ((bf16[88,64,88]{0,2,1:T(8,128)(2,1)}), bf16[88,64,88]{0,2,1:T(8,128)(2,1)}, u32[]{:S(2)}, u32[]{:S(2)}) async-start(bf16[88,64,88]{0,2,1:T(8,128)(2,1)} %bitcast.7), calls=%async_computation.2 | async-start | bytes 2883584 | tf_op jit(solution)/shard_map/all_to_all | solution.py:63
  586.8 12.8 %copy-start.6 = (bf16[88,7,1024]{2,1,0:T(8,128)(2,1)S(1)}, bf16[88,7,1024]{2,1,0:T(8,128)(2,1)}, u32[]{:S(2)}) copy-start(bf16[88,7,1024]{2,1,0:T(8,128)(2,1)} %copy-done.5) | copy-start | bytes 3784708
  586.8 206.3 %all-to-all-start.3 = ((bf16[64,19,1024]{2,1,0:T(8,128)(2,1)}), bf16[64,19,1024]{2,1,0:T(8,128)(2,1)}, u32[]{:S(2)}, u32[]{:S(2)}) async-start(bf16[64,19,1024]{2,1,0:T(8,128)(2,1)} %copy.32), calls=%async_computation.3 | async-start | bytes 6291456 | tf_op jit(solution)/shard_map/all_to_all | solution.py:79
  598.2 2.4 copy-start.4
  793.1 20.6 %copy-start.1 = (bf16[88,1024]{1,0:T(8,128)(2,1)S(1)}, bf16[88,1024]{1,0:T(8,128)(2,1)}, u32[]{:S(2)}) copy-start(bf16[88,1024]{1,0:T(8,128)(2,1)} %param.7) | copy-start | bytes 540676
Sparse Core Ops, SparseCore 0:
  9.8 324.7 all-gather.2
  344.1 69.2 all-reduce.2
  415.3 370.8 all-gather.4
where the time goes:
time: 824 us; the launch traced here: 820 us
  waiting for transfers between devices  555 us (67%)
  local copies, waits for them, and re-layouts  138 us (17%)
  blocking collectives  33.2 us (4%)
  other arithmetic  29.7 us (4%)
  starting transfers between devices  25.6 us (3%)
  matrix products  24.1 us (3%)
  between operations  14.1 us (2%)
    all_gather x1, waiting for transfers between devices, local(): every_passage = lax.all_gather(passages, 'dp', axis=0, tiled=True)  327 us
    all_gather x1, waiting for transfers between devices, local(): lax.all_gather(queries, 'dp', axis=0, tiled=True)  174 us
    scatter x2, local copies, waits for them, and re-layouts, local(): outgoing = jnp.zeros((dev_count, capacity, feature_count), jnp.bfloat16)....  65.2 us
    all_to_all x1, waiting for transfers between devices, local(): lax.all_to_all(found_rows, 'dp', split_axis=0, concat_axis=0, tiled=True)  53.3 us
    scatter x1, local copies, waits for them, and re-layouts, local(): requests = jnp.full((dev_count, capacity), row_count, jnp.int32).at[owner...  32.8 us
    all_to_all x1, blocking collectives, local(): lax.all_to_all(requests, 'dp', split_axis=0, concat_axis=0, tiled=True)  17.6 us
  transfers between devices with their start and end apart: 6, of which 3 were waited for; matrix products, arithmetic and copies ran while one was open for 19% of the time, Pallas kernels for 0%

commit v1 on v0

v1 whole, which is shorter than its diff:
```python
import functools

import jax
import jax.numpy as jnp
from jax import lax
from jax.experimental import pallas as pl
from jax.experimental.pallas import tpu as pltpu
from jax.sharding import Mesh, PartitionSpec as P

F32 = jnp.float32
BF16 = jnp.bfloat16
NEG = 7
ROWS = 88
FEAT = 1024
TOTAL = 8 * ROWS
QUARTER = 2 * ROWS
WIDE = 768
SCALE = 4096 ** (-0.5)
VMEM_LIMIT = 20 * 1024 * 1024
LAST = 640
NT = (((1,), (1,)), ((), ()))
NN = (((1,), (0,)), ((), ()))
TN = (((0,), (0,)), ((), ()))


def shift(x, axis, count, step):
    return lax.ppermute(x, axis, [(i, (i + step) % count) for i in range(count)])


def gather_z(x):
    half = 48
    r1 = shift(x, "z", 8, 1)
    l1 = shift(x, "z", 8, -1)
    r2 = shift(r1, "z", 8, 1)
    l2 = shift(l1, "z", 8, -1)
    r3 = shift(r2, "z", 8, 1)
    l3 = shift(l2, "z", 8, -1)
    r4 = shift(r3[:half], "z", 8, 1)
    l4 = shift(l3[half:], "z", 8, -1)
    return jnp.concatenate([x, r1, r2, r3, r4, l4, l3, l2, l1])


def prepare_kernel(q_ref, p_ref, n_ref, owner_ref, row_ref, q_out_ref, out_ref, turn_ref):
    q_out_ref[:, :FEAT] = q_ref[...]
    lane = lax.broadcasted_iota(jnp.int32, (ROWS, 128), 1)
    lane = lane.astype(F32)
    turn_ref[...] = jnp.zeros((128, 128), F32)
    turn_ref[:NEG, :ROWS] = owner_ref[...].astype(F32)
    turn_ref[8 : 8 + NEG, :ROWS] = row_ref[...].astype(F32)
    turned = jnp.transpose(turn_ref[...])[:ROWS]
    named = jnp.full((ROWS, 128), -1.0, F32)
    for k in range(NEG):
        named = jnp.where(lane == turned[:, k : k + 1], turned[:, 8 + k : 9 + k], named)
    q_out_ref[:, FEAT:] = named.astype(BF16)
    for b in range(8):
        out_ref[b, :, :FEAT] = p_ref[...]
        out_ref[b, :, FEAT:] = n_ref[...]


def position(*axes):
    return tuple(lax.axis_index(a) for a in axes)


def in_block(column, b):
    return (column >= b * ROWS) & (column < b * ROWS + ROWS)


def named_mask(names, z):
    owner = lax.broadcasted_iota(jnp.int32, (128, TOTAL), 0)
    column = lax.broadcasted_iota(jnp.int32, (128, TOTAL), 1)
    here = (owner < 64) & (((owner >> 1) & 7) == z)
    spot = (owner >> 4) * 2 + (owner & 1)
    spread = jnp.where(here & in_block(column, spot), 1.0, 0.0).astype(BF16)
    wanted = lax.dot_general(names, spread, NN, preferred_element_type=F32)
    inner = column[:8]
    for b in range(1, 8):
        inner = inner - jnp.where(column[:8] >= b * ROWS, ROWS, 0)
    return wanted == inner[:1].astype(F32), here, spot


def score_kernel(give, q_ref, pn_ref, out_ref):
    z, xh, core = position("z", "xh", "c")
    half = 1 - core if give else core
    mine = pl.ds(pl.multiple_of(half * 2 * QUARTER, 2 * QUARTER), 2 * QUARTER)
    names = q_ref[mine, FEAT:]
    mask, here, spot = named_mask(names, z)
    q = q_ref[mine, :FEAT]
    named = lax.dot_general(q, pn_ref[:, FEAT:], NT, preferred_element_type=F32)
    row = lax.broadcasted_iota(jnp.int32, (TOTAL, 128), 0)
    lane = lax.broadcasted_iota(jnp.int32, (TOTAL, 128), 1)
    gather = jnp.where((lane < 16) & in_block(row, lane & 7), 1.0, 0.0)
    value = lax.dot_general(
        jnp.where(mask, named, 0.0), gather, NN,
        precision=lax.Precision.HIGHEST, preferred_element_type=F32,
    )
    lane_b = lax.broadcasted_iota(jnp.int32, (128, 128), 1)
    pick = here[:, :128] & (spot[:, :128] == (lane_b & 7)) & (lane_b < 16)
    at_block = lax.dot_general(
        names, jnp.where(pick, 1.0, 0.0).astype(BF16), NN, preferred_element_type=F32
    )
    tail = jnp.where((at_block >= 0.0) & (lane[: 2 * QUARTER] < 16), value, -jnp.inf)
    scores = lax.dot_general(q, pn_ref[:, :FEAT], NT, preferred_element_type=F32)
    for j in range(2):
        slot = pl.ds(jnp.where(xh == j, 0, 1), 1)
        rows = slice(j * QUARTER, (j + 1) * QUARTER)
        out_ref[slot, :, :TOTAL] = scores[None, rows]
        out_ref[slot, :, TOTAL:] = tail[None, rows, : WIDE - TOTAL]


def soft_kernel(keep_ref, near_ref, far_ref, e_ref, stats_out_ref, turn_ref, stats_ref, sem):
    y, xl = position("y", "xl")
    scores = (keep_ref[0] + near_ref[0] + far_ref[0]) * SCALE
    peak = jnp.max(scores, axis=1, keepdims=True)
    e = jnp.exp(scores - peak)
    column = lax.broadcasted_iota(jnp.int32, scores.shape, 1)
    once = column < TOTAL + 8
    part = jnp.sum(jnp.where(once, e, 0.0), axis=1, keepdims=True)
    lane = lax.broadcasted_iota(jnp.int32, (QUARTER, 128), 1)
    column = lax.broadcasted_iota(jnp.int32, scores.shape, 1)
    row = lax.broadcasted_iota(jnp.int32, scores.shape, 0)
    own = (column == row + (y * 2 + xl) * ROWS) & (row < ROWS)
    positive = jnp.sum(jnp.where(own, scores, 0.0), axis=1, keepdims=True)
    info = jnp.where(lane == 0, peak, jnp.where(lane == 1, part, positive))
    stats_ref[...] = jnp.zeros(stats_ref.shape, F32)
    for h in range(2):
        turn_ref[...] = jnp.zeros((128, 128), F32)
        turn_ref[:ROWS, :] = info[h * ROWS : (h + 1) * ROWS]
        turned = jnp.transpose(turn_ref[...])
        for v in range(3):
            at = 2 * v + h
            stats_ref[:, at : at + 1, :] = jnp.broadcast_to(turned[None, v : v + 1], (32, 1, 128))
    copy = pltpu.make_async_copy(stats_ref, stats_out_ref, sem)
    copy.start()
    high = e.astype(BF16).astype(F32)
    e_ref[...] = jnp.where(once, high, e - high).astype(BF16)
    copy.wait()


PIECES = ((0, 0), (1, 0), (0, 1), (1, 1))


def per_quarter(xh, core, refs, body):
    for ref, (a, b) in zip(refs, PIECES):
        for quarter in range(4):
            c_of, x_of = quarter // 2, quarter % 2
            pl.when((core == (c_of ^ a)) & (xh == (x_of ^ b)))(functools.partial(body, ref, quarter))


def weight_kernel(
    stats_ref, e0_ref, e1_ref, e2_ref, e3_ref, pn_ref, q_far_ref,
    out_far_ref, gq_out_ref, loss_ref,
    out_ref, w_ref, high_ref, low_ref, gq_ref, mask_ref, q_ref,
    peak_ref, part_ref, turn_ref, sem,
):
    y, z, xl, xh, core = position("y", "z", "xl", "xh", "c")
    load = pltpu.make_async_copy(q_far_ref, q_ref, sem.at[0])
    load.start()
    for d in range(8):
        source = lax.rem(z + d, 8)
        for k in range(8):
            j = (k + d) % 8
            quarter, h = j // 2, j % 2
            c_from, x_from = quarter // 2, quarter % 2
            slot = source * 4 + (x_from * 2 + c_from)
            peak_ref[d, k : k + 1, :] = stats_ref[slot, h : h + 1, :]
            part_ref[d, k : k + 1, :] = stats_ref[slot, 2 + h : 3 + h, :]
    peaks = peak_ref[...]
    top = jnp.max(peaks, axis=0)
    whole = jnp.sum(part_ref[...] * jnp.exp(peaks - top[None]), axis=0)
    log_total = top + jnp.log(whole)
    positive = stats_ref[z * 4, 4:5, :]
    loss = log_total[0:1] - positive
    loss_ref[...] = jnp.broadcast_to(loss, (8, 128))
    turn_ref[...] = jnp.zeros((128, 128), F32)
    turn_ref[0:8, :] = jnp.exp(peaks[0] - log_total)
    turn_ref[8:9, :] = jnp.exp(-loss) - 1.0
    turned = jnp.transpose(turn_ref[...])
    column = lax.broadcasted_iota(jnp.int32, (ROWS, TOTAL), 1)
    row = lax.broadcasted_iota(jnp.int32, (ROWS, TOTAL), 0)
    diagonal = column == row + (y * 2 + xl) * ROWS

    lane = lax.broadcasted_iota(jnp.int32, (128, TOTAL), 0) - (TOTAL - LAST)
    wide = lax.broadcasted_iota(jnp.int32, (128, TOTAL), 1)
    spread = (lane >= 0) & (lane < 16) & in_block(wide, lane & 7)
    spread = jnp.where(spread, 1.0, 0.0).astype(BF16)

    def body(e_ref, quarter):
        rows = slice(quarter * QUARTER, (quarter + 1) * QUARTER)
        e = e_ref[:, :TOTAL].astype(F32)
        value = lax.dot_general(e_ref[:, LAST:], spread, NN, preferred_element_type=F32)
        value = value * mask_ref[rows, :].astype(F32)
        soft, named = [], []
        for h in range(2):
            k = 2 * quarter + h
            factor = turned[:ROWS, k : k + 1]
            part = e[h * ROWS : (h + 1) * ROWS] * factor
            if k == 0:
                part = jnp.where(diagonal, turned[:ROWS, 8:9], part)
            soft.append(part)
            named.append(value[h * ROWS : (h + 1) * ROWS] * factor)
        w_ref[rows, :] = jnp.concatenate(soft).astype(BF16)
        value = jnp.concatenate(named)
        high = value.astype(BF16)
        high_ref[rows, :] = high
        low_ref[rows, :] = (value - high.astype(F32)).astype(BF16)

    load.wait()
    mask_ref[...] = jnp.where(named_mask(q_ref[:, FEAT:], z)[0], 1.0, 0.0).astype(BF16)
    pieces = ((e0_ref, 0, 0), (e1_ref, 1, 0), (e2_ref, 0, 1), (e3_ref, 1, 1))
    for e_ref, a, b in pieces:
        for quarter in range(4):
            c_of, x_of = quarter // 2, quarter % 2
            here = (core == (c_of ^ a)) & (xh == (x_of ^ b))
            pl.when(here)(functools.partial(body, e_ref, quarter))

    def dot(a, b, dims):
        return lax.dot_general(a, b, dims, preferred_element_type=F32)

    gq = dot(w_ref[...], pn_ref[:, :FEAT], NN) + dot(high_ref[...], pn_ref[:, FEAT:], NN)
    gq = SCALE * gq
    for k in range(8):
        gq_ref[pl.ds(lax.rem(z - k + 8, 8), 1)] = gq[None, k * ROWS : (k + 1) * ROWS]
    copy = pltpu.make_async_copy(gq_ref, gq_out_ref, sem.at[1])
    copy.start()
    q = q_ref[:, :FEAT]
    out_ref[:, :FEAT] = (SCALE * dot(w_ref[...], q, TN)).astype(BF16)
    front = pltpu.make_async_copy(out_ref.at[:, :FEAT], out_far_ref.at[:, :FEAT], sem.at[2])
    front.start()
    gn = dot(high_ref[...], q, TN) + dot(low_ref[...], q, TN)
    out_ref[:, FEAT:] = (SCALE * gn).astype(BF16)
    back = pltpu.make_async_copy(out_ref.at[:, FEAT:], out_far_ref.at[:, FEAT:], sem.at[3])
    back.start()
    copy.wait()
    front.wait()
    back.wait()


def finish_kernel(gq_ref, x_ref, gq_out_ref, gp_out_ref, gn_out_ref):
    gq_out_ref[...] = gq_ref[...].astype(BF16)
    for first, out_ref in ((0, gp_out_ref), (FEAT, gn_out_ref)):
        total = x_ref[0, :, first : first + FEAT].astype(F32)
        for b in range(1, 8):
            total += x_ref[b, :, first : first + FEAT].astype(F32)
        out_ref[...] = total.astype(BF16)


def call(kernel, name, operands, outs, scratch=(), far_in=0, far_out=(), limit=20):
    vmem = pl.BlockSpec(memory_space=pltpu.VMEM)
    hbm = pl.BlockSpec(memory_space=pltpu.HBM)
    return pl.pallas_call(
        kernel,
        out_shape=outs,
        in_specs=[vmem] * (len(operands) - far_in) + [hbm] * far_in,
        out_specs=tuple(hbm if i in far_out else vmem for i in range(len(outs))),
        scratch_shapes=scratch,
        compiler_params=pltpu.CompilerParams(vmem_limit_bytes=limit * 1024 * 1024),
        cost_estimate=pl.CostEstimate(flops=0, bytes_accessed=1024, transcendentals=0),
        name=name,
    )(*operands)


def shaped(shape, dtype):
    return jax.ShapeDtypeStruct(shape, dtype)


def local(queries, passages, negatives, neg_owner, neg_row):
    plane = ("y", "xl")

    packed, spread = pl.pallas_call(
        prepare_kernel,
        out_shape=(shaped((ROWS, FEAT + 128), BF16), shaped((8, ROWS, 2 * FEAT), BF16)),
        compiler_params=pltpu.CompilerParams(vmem_limit_bytes=60 * 1024 * 1024),
        grid=(1,),
        in_specs=[pl.BlockSpec((ROWS, FEAT), lambda i: (0, 0))] * 3
        + [pl.BlockSpec((NEG, ROWS), lambda i: (0, 0))] * 2,
        out_specs=(
            pl.BlockSpec((ROWS, FEAT + 128), lambda i: (0, 0)),
            pl.BlockSpec((8, ROWS, 2 * FEAT), lambda i: (0, 0, 0)),
        ),
        scratch_shapes=[pltpu.VMEM((128, 128), F32)],
        name="prepare",
    )(queries, passages, negatives, neg_owner.T, neg_row.T)
    pn = lax.all_to_all(spread, plane, 0, 0, tiled=True).reshape(TOTAL, 2 * FEAT)
    q_cat = gather_z(packed)

    def scores_half(give):
        return call(
            functools.partial(score_kernel, give), "scores_give" if give else "scores_keep",
            (q_cat, pn), (shaped((2, QUARTER, WIDE), F32),),
        )[0]

    give = scores_half(True)
    near = shift(give, "c", 2, 1)
    keep = scores_half(False)
    far = shift(keep[1:] + near[1:], "xh", 2, 1)

    e0, stats = call(
        soft_kernel, "soft", (keep, near, far),
        (shaped((QUARTER, WIDE), BF16), shaped((32, 8, 128), F32)),
        [pltpu.VMEM((128, 128), F32), pltpu.VMEM((32, 8, 128), F32), pltpu.SemaphoreType.DMA],
        far_out=(1,),
    )
    stats = lax.all_to_all(stats, ("z", "xh", "c"), 0, 0, tiled=True)
    e2 = shift(e0, "xh", 2, 1)
    e1 = shift(e0, "c", 2, 1)
    e2, stats = lax.optimization_barrier((e2, stats))
    e3 = shift(e2, "c", 2, 1)

    gpn, gq, loss = call(
        weight_kernel, "weights",
        (stats, e0, e1, e2, e3, pn, q_cat),
        (
            shaped((TOTAL, 2 * FEAT), BF16), shaped((8, ROWS, FEAT), F32), shaped((8, 128), F32),
        ),
        [pltpu.VMEM((TOTAL, 2 * FEAT), BF16)]
        + [pltpu.VMEM((TOTAL, TOTAL), BF16)] * 3
        + [pltpu.VMEM((8, ROWS, FEAT), F32)]
        + [pltpu.VMEM((TOTAL, TOTAL), BF16), pltpu.VMEM((TOTAL, FEAT + 128), BF16)]
        + [pltpu.VMEM((8, 8, 128), F32)] * 2
        + [pltpu.VMEM((128, 128), F32), pltpu.SemaphoreType.DMA((4,))],
        far_in=1,
        far_out=(0, 1),
        limit=58,
    )
    grad_queries = lax.psum_scatter(gq, "z", scatter_dimension=0, tiled=True)[0]
    gpn = lax.all_to_all(gpn.reshape(8, ROWS, 2 * FEAT), plane, 0, 0, tiled=True)

    vmem = pl.BlockSpec(memory_space=pltpu.VMEM)
    grads = pl.pallas_call(
        finish_kernel,
        out_shape=(shaped((ROWS, FEAT), BF16),) * 3,
        grid=(1,),
        in_specs=[vmem, vmem],
        out_specs=(pl.BlockSpec((ROWS, FEAT), lambda i: (0, 0)),) * 3,
        compiler_params=pltpu.CompilerParams(vmem_limit_bytes=VMEM_LIMIT),
        name="finish",
    )(grad_queries, gpn)
    return (loss[0, :ROWS],) + tuple(grads)


def solution(mesh):
    fine = Mesh(mesh.devices.reshape(4, 8, 2, 2, 2), ("y", "z", "xl", "xh", "c"))
    dp, width = ("y", "z", "xl"), ("xh", "c")
    in_specs = (P(dp, width), P(dp, width), P(dp, width), P(dp, None), P(dp, None))
    out_specs = (P(dp), P(dp, width), P(dp, width), P(dp, width))
    return jax.shard_map(local, mesh=fine, in_specs=in_specs, out_specs=out_specs, check_vma=False)
```

time: 824 us -> 164 us (0.20)
  waiting for transfers between devices: 555 us -> 76.7 us
  local copies, waits for them, and re-layouts: 138 us -> 6.73 us
  blocking collectives: 33.2 us -> 0 us
  other arithmetic: 29.7 us -> 0.06 us
  matrix products: 24.1 us -> 0 us
  Pallas kernels: 0 us -> 23.4 us
  starting transfers between devices: 25.6 us -> 40.4 us
    all_gather x2 -> x0, waiting for transfers between devices: 500 us -> none  [the longest x1 327 us: local(): every_passage = lax.all_gather(passages, 'dp', axis=0, tiled=True)]
    scatter x3 -> x0, local copies, waits for them, and re-layouts: 98 us -> none  [the longest x2 65.2 us: local(): outgoing = jnp.zeros((dev_count, capacity, feature_count), jnp.bfloat16)....]
    ppermute x0 -> x13, waiting for transfers between devices: none -> 31.1 us  [shift(): lax.ppermute(x, axis, [(i, (i + step) % count) for i in range(count)])]
    dot_general x4 -> x0, matrix products: 24.1 us -> none  [the longest x1 9.28 us: local(): jnp.einsum('qd,pd->qp', queries, every_passage, preferred_element_type=jn...]
    ppermute x0 -> x13, starting transfers between devices: none -> 23.8 us  [shift(): lax.ppermute(x, axis, [(i, (i + step) % count) for i in range(count)])]
    pallas_call x0 -> x6, Pallas kernels: none -> 23.4 us  [the longest x4 19.1 us: call(): pl.pallas_call(kernel, out_shape=outs, in_specs=[vmem] * (len(operands) -...]
    gather x3 -> x0, local copies, waits for them, and re-layouts: 18.7 us -> none  [the longest x1 11.8 us: local(): fetched[owner_flat, slot_index].reshape(row_count, neg_count, feature_count)]
    all_to_all x1 -> x0, blocking collectives: 17.6 us -> none  [local(): lax.all_to_all(requests, 'dp', split_axis=0, concat_axis=0, tiled=True)]
  transfers between devices with their start and end apart: 6 -> 17, of which waited for: 3 -> 10; matrix products, arithmetic and copies ran while one was open for 19% -> 1% of each run, Pallas kernels for 0% -> 2%
where the time goes in v1:
time: 164 us; the launch traced here: 161 us
  waiting for transfers between devices  76.7 us (47%)
  starting transfers between devices  40.4 us (25%)
  Pallas kernels  23.4 us (14%)
  between operations  14.2 us (9%)
  local copies, waits for them, and re-layouts  6.73 us (4%)
    all_to_all x1, waiting for transfers between devices, local(): lax.all_to_all(gpn.reshape(8, ROWS, 2 * FEAT), plane, 0, 0, tiled=True)  34.8 us
    ppermute x13, waiting for transfers between devices, shift(): lax.ppermute(x, axis, [(i, (i + step) % count) for i in range(count)])  31.1 us
    ppermute x13, starting transfers between devices, shift(): lax.ppermute(x, axis, [(i, (i + step) % count) for i in range(count)])  23.8 us
    pallas_call x4, Pallas kernels, call(): pl.pallas_call(kernel, out_shape=outs, in_specs=[vmem] * (len(operands) -...  19.1 us
    all_to_all x1, waiting for transfers between devices, local(): stats = lax.all_to_all(stats, ('z', 'xh', 'c'), 0, 0, tiled=True)  10.3 us
    all_to_all x1, starting transfers between devices, local(): stats = lax.all_to_all(stats, ('z', 'xh', 'c'), 0, 0, tiled=True)  9.1 us
    unnamed x28, local copies, waits for them, and re-layouts  5.49 us
    all_to_all x1, starting transfers between devices, local(): lax.all_to_all(spread, plane, 0, 0, tiled=True).reshape(TOTAL, 2 * FEAT)  3.79 us
  transfers between devices with their start and end apart: 17, of which 10 were waited for; matrix products, arithmetic and copies ran while one was open for 1% of the time, Pallas kernels for 2%

profile of v1, /device:TPU:0, one launch (start us, length us, event | category | flops | bytes accessed | tf_op | source)
XLA Modules:
  0.0 161.5 jit_solution(17500852523197054166)
XLA Ops:
  7.2 3.2 %prepare.1 = (bf16[88,1152]{1,0:T(8,128)(2,1)}, bf16[8,88,2048]{2,1,0:T(8,128)(2,1)}) custom-call(bf16[88,1024]{1,0:T(8,128)(2,1)} %q_ref.1, bf16[88,1024]{1,0:T(8,128)(2,1)} %p_ref.1, bf16[88,1024]{1,0:T(8,128)(2,1)} %n_ref.1, s32[7,88]{1,0:T(8,128)} %bitcast.12, s32[7,88]{1,0:T(8,128)} %bitcast.13), custom_call_target="tpu_custom_call" | custom-call | tf_op jit(solution)/shard_map/prepare/pallas_call | solution.py:269
  10.3 0.0 copy-start.9
  10.3 3.8 %all-to-all-start = ((bf16[8,88,2048]{2,1,0:T(8,128)(2,1)}), bf16[8,88,2048]{2,1,0:T(8,128)(2,1)S(1)}, u32[]{:S(2)}, u32[]{:S(2)}) async-start(bf16[8,88,2048]{2,1,0:T(8,128)(2,1)} %get-tuple-element.17), calls=%async_computation | async-start | bytes 5767168 | tf_op jit(solution)/shard_map/all_to_all | solution.py:283
  14.1 0.0 copy-done.9
  14.1 5.9 %collective-permute-start.4 = (bf16[88,1152]{1,0:T(8,128)(2,1)S(1)}, bf16[88,1152]{1,0:T(8,128)(2,1)S(1)}, u32[]{:S(2)}, u32[]{:S(2)}) collective-permute-start(bf16[88,1152]{1,0:T(8,128)(2,1)S(1)} %copy-done.9), channel_id=1, source_target_pairs={{0,56},{8,0},{16,8},{24,16},{32,24},{40,32},{48,40},{56,48},{1,57}... | collective-permute-start | bytes 608264 | tf_op jit(solution)/shard_map/ppermute | solution.py:27
  20.1 0.0 collective-permute-start
  20.1 4.0 %collective-permute-done.4 = bf16[88,1152]{1,0:T(8,128)(2,1)S(1)} collective-permute-done((bf16[88,1152]{1,0:T(8,128)(2,1)S(1)}, bf16[88,1152]{1,0:T(8,128)(2,1)S(1)}, u32[]{:S(2)}, u32[]{:S(2)}) %collective-permute-start.4) | collective-permute-done | bytes 202784 | tf_op jit(solution)/shard_map/ppermute | solution.py:27
  24.1 3.7 %collective-permute-start.5 = (bf16[88,1152]{1,0:T(8,128)(2,1)S(1)}, bf16[88,1152]{1,0:T(8,128)(2,1)S(1)}, u32[]{:S(2)}, u32[]{:S(2)}) collective-permute-start(bf16[88,1152]{1,0:T(8,128)(2,1)S(1)} %collective-permute-done.4), channel_id=1, source_target_pairs={{0,56},{8,0},{16,8},{24,16},{32,24},{40,32},{48,40},{56,48},{1,57}... | collective-permute-start | bytes 608264 | tf_op jit(solution)/shard_map/ppermute | solution.py:27
  27.8 0.0 collective-permute-done
  27.8 0.0 collective-permute-start.1
  27.8 3.2 %collective-permute-done.5 = bf16[88,1152]{1,0:T(8,128)(2,1)S(1)} collective-permute-done((bf16[88,1152]{1,0:T(8,128)(2,1)S(1)}, bf16[88,1152]{1,0:T(8,128)(2,1)S(1)}, u32[]{:S(2)}, u32[]{:S(2)}) %collective-permute-start.5) | collective-permute-done | bytes 202784 | tf_op jit(solution)/shard_map/ppermute | solution.py:27
  31.0 3.7 %collective-permute-start.6 = (bf16[88,1152]{1,0:T(8,128)(2,1)S(1)}, bf16[88,1152]{1,0:T(8,128)(2,1)S(1)}, u32[]{:S(2)}, u32[]{:S(2)}) collective-permute-start(bf16[88,1152]{1,0:T(8,128)(2,1)S(1)} %collective-permute-done.5), channel_id=1, source_target_pairs={{0,56},{8,0},{16,8},{24,16},{32,24},{40,32},{48,40},{56,48},{1,57}... | collective-permute-start | bytes 608264 | tf_op jit(solution)/shard_map/ppermute | solution.py:27
  34.7 0.0 collective-permute-done.1
  34.7 0.0 collective-permute-start.2
  34.8 3.2 %collective-permute-done.6 = bf16[88,1152]{1,0:T(8,128)(2,1)S(1)} collective-permute-done((bf16[88,1152]{1,0:T(8,128)(2,1)S(1)}, bf16[88,1152]{1,0:T(8,128)(2,1)S(1)}, u32[]{:S(2)}, u32[]{:S(2)}) %collective-permute-start.6) | collective-permute-done | bytes 202784 | tf_op jit(solution)/shard_map/ppermute | solution.py:27
  38.0 3.8 %collective-permute-start.7 = (bf16[40,1152]{1,0:T(8,128)(2,1)S(1)}, bf16[40,1152]{1,0:T(8,128)(2,1)S(1)}, u32[]{:S(2)}, u32[]{:S(2)}) collective-permute-start(bf16[40,1152]{1,0:T(8,128)(2,1)S(1)} %slice.21), channel_id=1, source_target_pairs={{0,56},{8,0},{16,8},{24,16},{32,24},{40,32},{48,40},{56,48},{1,57}... | collective-permute-start | bytes 276488 | tf_op jit(solution)/shard_map/ppermute | solution.py:27
  41.8 0.0 collective-permute-done.2
  41.8 0.1 collective-permute-start.3
  41.9 5.9 %collective-permute-done.3 = bf16[48,1152]{1,0:T(8,128)(2,1)S(1)} collective-permute-done((bf16[48,1152]{1,0:T(8,128)(2,1)S(1)}, bf16[48,1152]{1,0:T(8,128)(2,1)S(1)}, u32[]{:S(2)}, u32[]{:S(2)}) %collective-permute-start.3) | collective-permute-done | bytes 110624 | tf_op jit(solution)/shard_map/ppermute | solution.py:27
  47.8 0.0 collective-permute-done.7
  48.0 0.0 copy-start.1
  48.0 1.2 copy-done.1
  49.1 0.4 all-to-all-done
  49.5 0.0 copy-start
  49.5 0.0 copy-start.2
  49.5 2.5 %copy-done.2 = bf16[704,1152]{1,0:T(8,128)(2,1)S(1)} copy-done((bf16[704,1152]{1,0:T(8,128)(2,1)S(1)}, bf16[704,1152]{1,0:T(8,128)(2,1)}, u32[]{:S(2)}) %copy-start.2) | copy-done | bytes 1622040
  52.0 2.5 %scores_give.1 = f32[2,176,768]{2,1,0:T(8,128)S(1)} custom-call(bf16[704,1152]{1,0:T(8,128)(2,1)S(1)} %copy-done.2, bf16[704,2048]{1,0:T(8,128)(2,1)S(1)} %bitcast.7), custom_call_target="tpu_custom_call" | custom-call | bytes 1024 | tf_op jit(solution)/shard_map/scores_give/pallas_call | solution.py:250
  54.6 0.3 collective-permute-start.8
  54.8 0.0 copy-done
  54.9 2.5 %scores_keep.1.keep_ref = f32[2,176,768]{2,1,0:T(8,128)S(1)} custom-call(bf16[704,1152]{1,0:T(8,128)(2,1)S(1)} %copy-done.2, bf16[704,2048]{1,0:T(8,128)(2,1)S(1)} %bitcast.8), custom_call_target="tpu_custom_call" | custom-call | bytes 1024 | tf_op jit(solution)/shard_map/scores_keep/pallas_call | solution.py:250
  57.4 0.2 collective-permute-done.8.near_ref
  57.5 0.1 slice_add_fusion
  57.6 2.8 %collective-permute-start.9 = (f32[1,176,768]{2,1,0:T(8,128)S(1)}, f32[1,176,768]{2,1,0:T(8,128)S(1)}, u32[]{:S(2)}, u32[]{:S(2)}) collective-permute-start(f32[1,176,768]{2,1,0:T(8,128)S(1)} %slice_add_fusion), channel_id=1, source_target_pairs={{0,2},{2,0},{1,3},{3,1},{4,6},{6,4},{5,7},{7,5},{8,10},{10,8},{9,1... | collective-permute-start | bytes 1622024 | tf_op jit(solution)/shard_map/ppermute | solution.py:27
  60.4 13.3 %collective-permute-done.9.far_ref = f32[1,176,768]{2,1,0:T(8,128)S(1)} collective-permute-done((f32[1,176,768]{2,1,0:T(8,128)S(1)}, f32[1,176,768]{2,1,0:T(8,128)S(1)}, u32[]{:S(2)}, u32[]{:S(2)}) %collective-permute-start.9) | collective-permute-done | bytes 540704 | tf_op jit(solution)/shard_map/ppermute | solution.py:27
  73.7 1.1 soft.1
  74.8 0.0 copy-start.4
  74.8 2.8 %collective-permute-start.10 = (bf16[176,768]{1,0:T(8,128)(2,1)S(1)}, bf16[176,768]{1,0:T(8,128)(2,1)S(1)}, u32[]{:S(2)}, u32[]{:S(2)}) collective-permute-start(bf16[176,768]{1,0:T(8,128)(2,1)S(1)} %get-tuple-element.18.e0_ref), channel_id=1, source_target_pairs={{0,2},{2,0},{1,3},{3,1},{4,6},{6,4},{5,7},{7,5},{8,10},{10,8},{9,1... | collective-permute-start | bytes 811016 | tf_op jit(solution)/shard_map/ppermute | solution.py:27
  77.6 9.1 %all-to-all-start.1 = ((f32[32,8,128]{2,1,0:T(8,128)}), f32[32,8,128]{2,1,0:T(8,128)S(1)}, u32[]{:S(2)}, u32[]{:S(2)}) async-start(f32[32,8,128]{2,1,0:T(8,128)} %get-tuple-element.19), calls=%async_computation.1 | async-start | bytes 262144 | tf_op jit(solution)/shard_map/all_to_all | solution.py:303
  86.7 0.0 reduce-scatter.2.cloned.1.call-start
  86.8 0.4 collective-permute-start.11
  87.1 10.3 %all-to-all-done.1.stats_ref = f32[32,8,128]{2,1,0:T(8,128)S(1)} async-done(((f32[32,8,128]{2,1,0:T(8,128)}), f32[32,8,128]{2,1,0:T(8,128)S(1)}, u32[]{:S(2)}, u32[]{:S(2)}) %all-to-all-start.1) | async-done | bytes 131104 | tf_op jit(solution)/shard_map/all_to_all | solution.py:303
  97.5 0.0 copy-start.5
  97.5 0.0 collective-permute-done.10.e2_ref
  97.5 0.0 copy-start.6
  97.5 0.4 collective-permute-start.12
  97.9 0.0 collective-permute-done.11.e1_ref
  97.9 0.0 copy-start.7
  97.9 1.3 collective-permute-done.12.e3_ref
  99.1 0.0 copy-done.4
  99.1 0.0 copy-done.5
  99.1 0.0 copy-done.6
  99.1 0.0 copy-done.7
  99.1 0.0 copy-start.8
  99.2 0.7 copy-done.8
  99.9 13.0 %weights.1 = (bf16[704,2048]{1,0:T(8,128)(2,1)}, f32[8,88,1024]{2,1,0:T(8,128)}, f32[8,128]{1,0:T(8,128)}) custom-call(f32[32,8,128]{2,1,0:T(8,128)} %copy-done.5, bf16[176,768]{1,0:T(8,128)(2,1)} %copy-done.4, bf16[176,768]{1,0:T(8,128)(2,1)} %copy-done.7, bf16[176,768]{1,0:T(8,128)(2,1)} %copy-done.6, bf16[176,768]{1,0:T(8,128)(2,1)} %copy-done.8, ...), custom_call_target="tpu_custom_call" | custom-call | bytes 1024 | tf_op jit(solution)/shard_map/weights/pallas_call | solution.py:250
  112.9 0.0 reduce-scatter.2.cloned.1.call-update
  112.9 3.6 %all-to-all-start.2 = ((bf16[8,88,2048]{2,1,0:T(8,128)(2,1)}), bf16[8,88,2048]{2,1,0:T(8,128)(2,1)S(1)}, u32[]{:S(2)}, u32[]{:S(2)}) async-start(bf16[8,88,2048]{2,1,0:T(8,128)(2,1)} %bitcast.11), calls=%async_computation.3 | async-start | bytes 5767168 | tf_op jit(solution)/shard_map/all_to_all | solution.py:326
  116.6 1.2 slice_bitcast_fusion
  117.8 34.8 %all-to-all-done.2.x_ref = bf16[8,88,2048]{2,1,0:T(8,128)(2,1)S(1)} async-done(((bf16[8,88,2048]{2,1,0:T(8,128)(2,1)}), bf16[8,88,2048]{2,1,0:T(8,128)(2,1)S(1)}, u32[]{:S(2)}, u32[]{:S(2)}) %all-to-all-start.2) | async-done | bytes 2883616 | tf_op jit(solution)/shard_map/all_to_all | solution.py:326
  152.6 0.0 reduce-scatter.2.cloned.1.call-done
  152.6 0.0 copy-start.3
  152.6 1.0 copy-done.3
  153.6 1.0 finish.1
  (11 shorter events, 0.2 us)
Async XLA Ops:
  10.3 3.8 %copy-start.9 = (bf16[88,1152]{1,0:T(8,128)(2,1)S(1)}, bf16[88,1152]{1,0:T(8,128)(2,1)}, u32[]{:S(2)}) copy-start(bf16[88,1152]{1,0:T(8,128)(2,1)} %get-tuple-element.16) | copy-start | bytes 608260
  10.3 39.2 %all-to-all-start = ((bf16[8,88,2048]{2,1,0:T(8,128)(2,1)}), bf16[8,88,2048]{2,1,0:T(8,128)(2,1)S(1)}, u32[]{:S(2)}, u32[]{:S(2)}) async-start(bf16[8,88,2048]{2,1,0:T(8,128)(2,1)} %get-tuple-element.17), calls=%async_computation | async-start | bytes 5767168 | tf_op jit(solution)/shard_map/all_to_all | solution.py:283
  14.1 9.9 %collective-permute-start.4 = (bf16[88,1152]{1,0:T(8,128)(2,1)S(1)}, bf16[88,1152]{1,0:T(8,128)(2,1)S(1)}, u32[]{:S(2)}, u32[]{:S(2)}) collective-permute-start(bf16[88,1152]{1,0:T(8,128)(2,1)S(1)} %copy-done.9), channel_id=1, source_target_pairs={{0,56},{8,0},{16,8},{24,16},{32,24},{40,32},{48,40},{56,48},{1,57}... | collective-permute-start | bytes 608264 | tf_op jit(solution)/shard_map/ppermute | solution.py:27
  20.1 7.7 %collective-permute-start = (bf16[88,1152]{1,0:T(8,128)(2,1)S(1)}, bf16[88,1152]{1,0:T(8,128)(2,1)S(1)}, u32[]{:S(2)}, u32[]{:S(2)}) collective-permute-start(bf16[88,1152]{1,0:T(8,128)(2,1)S(1)} %copy-done.9), channel_id=1, source_target_pairs={{0,8},{8,16},{16,24},{24,32},{32,40},{40,48},{48,56},{56,0},{1,9},... | collective-permute-start | bytes 608264 | tf_op jit(solution)/shard_map/ppermute | solution.py:27
  24.1 6.9 %collective-permute-start.5 = (bf16[88,1152]{1,0:T(8,128)(2,1)S(1)}, bf16[88,1152]{1,0:T(8,128)(2,1)S(1)}, u32[]{:S(2)}, u32[]{:S(2)}) collective-permute-start(bf16[88,1152]{1,0:T(8,128)(2,1)S(1)} %collective-permute-done.4), channel_id=1, source_target_pairs={{0,56},{8,0},{16,8},{24,16},{32,24},{40,32},{48,40},{56,48},{1,57}... | collective-permute-start | bytes 608264 | tf_op jit(solution)/shard_map/ppermute | solution.py:27
  27.8 6.9 %collective-permute-start.1 = (bf16[88,1152]{1,0:T(8,128)(2,1)S(1)}, bf16[88,1152]{1,0:T(8,128)(2,1)S(1)}, u32[]{:S(2)}, u32[]{:S(2)}) collective-permute-start(bf16[88,1152]{1,0:T(8,128)(2,1)S(1)} %collective-permute-done), channel_id=1, source_target_pairs={{0,8},{8,16},{16,24},{24,32},{32,40},{40,48},{48,56},{56,0},{1,9},... | collective-permute-start | bytes 608264 | tf_op jit(solution)/shard_map/ppermute | solution.py:27
  31.0 6.9 %collective-permute-start.6 = (bf16[88,1152]{1,0:T(8,128)(2,1)S(1)}, bf16[88,1152]{1,0:T(8,128)(2,1)S(1)}, u32[]{:S(2)}, u32[]{:S(2)}) collective-permute-start(bf16[88,1152]{1,0:T(8,128)(2,1)S(1)} %collective-permute-done.5), channel_id=1, source_target_pairs={{0,56},{8,0},{16,8},{24,16},{32,24},{40,32},{48,40},{56,48},{1,57}... | collective-permute-start | bytes 608264 | tf_op jit(solution)/shard_map/ppermute | solution.py:27
  34.7 7.0 %collective-permute-start.2 = (bf16[88,1152]{1,0:T(8,128)(2,1)S(1)}, bf16[88,1152]{1,0:T(8,128)(2,1)S(1)}, u32[]{:S(2)}, u32[]{:S(2)}) collective-permute-start(bf16[88,1152]{1,0:T(8,128)(2,1)S(1)} %collective-permute-done.1), channel_id=1, source_target_pairs={{0,8},{8,16},{16,24},{24,32},{32,40},{40,48},{48,56},{56,0},{1,9},... | collective-permute-start | bytes 608264 | tf_op jit(solution)/shard_map/ppermute | solution.py:27
  38.0 9.8 %collective-permute-start.7 = (bf16[40,1152]{1,0:T(8,128)(2,1)S(1)}, bf16[40,1152]{1,0:T(8,128)(2,1)S(1)}, u32[]{:S(2)}, u32[]{:S(2)}) collective-permute-start(bf16[40,1152]{1,0:T(8,128)(2,1)S(1)} %slice.21), channel_id=1, source_target_pairs={{0,56},{8,0},{16,8},{24,16},{32,24},{40,32},{48,40},{56,48},{1,57}... | collective-permute-start | bytes 276488 | tf_op jit(solution)/shard_map/ppermute | solution.py:27
  41.8 6.0 %collective-permute-start.3 = (bf16[48,1152]{1,0:T(8,128)(2,1)S(1)}, bf16[48,1152]{1,0:T(8,128)(2,1)S(1)}, u32[]{:S(2)}, u32[]{:S(2)}) collective-permute-start(bf16[48,1152]{1,0:T(8,128)(2,1)S(1)} %slice.20), channel_id=1, source_target_pairs={{0,8},{8,16},{16,24},{24,32},{32,40},{40,48},{48,56},{56,0},{1,9},... | collective-permute-start | bytes 331784 | tf_op jit(solution)/shard_map/ppermute | solution.py:27
  48.0 1.2 copy-start.1
  49.5 5.3 %copy-start = (bf16[8,88,2048]{2,1,0:T(8,128)(2,1)}, bf16[8,88,2048]{2,1,0:T(8,128)(2,1)S(1)}, u32[]{:S(2)}) copy-start(bf16[8,88,2048]{2,1,0:T(8,128)(2,1)S(1)} %all-to-all-done) | copy-start | bytes 8650756
  49.5 2.5 %copy-start.2 = (bf16[704,1152]{1,0:T(8,128)(2,1)S(1)}, bf16[704,1152]{1,0:T(8,128)(2,1)}, u32[]{:S(2)}) copy-start(bf16[704,1152]{1,0:T(8,128)(2,1)} %copy-done.1) | copy-start | bytes 4866052
  54.6 3.0 %collective-permute-start.8 = (f32[2,176,768]{2,1,0:T(8,128)S(1)}, f32[2,176,768]{2,1,0:T(8,128)S(1)}, u32[]{:S(2)}, u32[]{:S(2)}) collective-permute-start(f32[2,176,768]{2,1,0:T(8,128)S(1)} %scores_give.1), channel_id=1, source_target_pairs={{0,1},{1,0},{2,3},{3,2},{4,5},{5,4},{6,7},{7,6},{8,9},{9,8},{10,11... | collective-permute-start | bytes 3244040 | tf_op jit(solution)/shard_map/ppermute | solution.py:27
  57.6 16.1 %collective-permute-start.9 = (f32[1,176,768]{2,1,0:T(8,128)S(1)}, f32[1,176,768]{2,1,0:T(8,128)S(1)}, u32[]{:S(2)}, u32[]{:S(2)}) collective-permute-start(f32[1,176,768]{2,1,0:T(8,128)S(1)} %slice_add_fusion), channel_id=1, source_target_pairs={{0,2},{2,0},{1,3},{3,1},{4,6},{6,4},{5,7},{7,5},{8,10},{10,8},{9,1... | collective-permute-start | bytes 1622024 | tf_op jit(solution)/shard_map/ppermute | solution.py:27
  74.8 24.3 %copy-start.4 = (bf16[176,768]{1,0:T(8,128)(2,1)}, bf16[176,768]{1,0:T(8,128)(2,1)S(1)}, u32[]{:S(2)}) copy-start(bf16[176,768]{1,0:T(8,128)(2,1)S(1)} %get-tuple-element.18.e0_ref) | copy-start | bytes 811012
  74.8 22.7 %collective-permute-start.10 = (bf16[176,768]{1,0:T(8,128)(2,1)S(1)}, bf16[176,768]{1,0:T(8,128)(2,1)S(1)}, u32[]{:S(2)}, u32[]{:S(2)}) collective-permute-start(bf16[176,768]{1,0:T(8,128)(2,1)S(1)} %get-tuple-element.18.e0_ref), channel_id=1, source_target_pairs={{0,2},{2,0},{1,3},{3,1},{4,6},{6,4},{5,7},{7,5},{8,10},{10,8},{9,1... | collective-permute-start | bytes 811016 | tf_op jit(solution)/shard_map/ppermute | solution.py:27
  77.6 19.9 %all-to-all-start.1 = ((f32[32,8,128]{2,1,0:T(8,128)}), f32[32,8,128]{2,1,0:T(8,128)S(1)}, u32[]{:S(2)}, u32[]{:S(2)}) async-start(f32[32,8,128]{2,1,0:T(8,128)} %get-tuple-element.19), calls=%async_computation.1 | async-start | bytes 262144 | tf_op jit(solution)/shard_map/all_to_all | solution.py:303
  86.7 65.9 %reduce-scatter.2.cloned.1.call-start = ((), (), s32[]{:S(2)}) async-start(), calls=%async_computation.4 | async-start | bytes 3244032 | tf_op jit(solution)/shard_map/reduce_scatter | solution.py:325
  86.8 11.1 %collective-permute-start.11 = (bf16[176,768]{1,0:T(8,128)(2,1)S(1)}, bf16[176,768]{1,0:T(8,128)(2,1)S(1)}, u32[]{:S(2)}, u32[]{:S(2)}) collective-permute-start(bf16[176,768]{1,0:T(8,128)(2,1)S(1)} %get-tuple-element.18.e0_ref), channel_id=1, source_target_pairs={{0,1},{1,0},{2,3},{3,2},{4,5},{5,4},{6,7},{7,6},{8,9},{9,8},{10,11... | collective-permute-start | bytes 811016 | tf_op jit(solution)/shard_map/ppermute | solution.py:27
  97.5 1.6 %copy-start.5 = (f32[32,8,128]{2,1,0:T(8,128)}, f32[32,8,128]{2,1,0:T(8,128)S(1)}, u32[]{:S(2)}) copy-start(f32[32,8,128]{2,1,0:T(8,128)S(1)} %all-to-all-done.1.stats_ref) | copy-start | bytes 393220
  97.5 1.6 %copy-start.6 = (bf16[176,768]{1,0:T(8,128)(2,1)}, bf16[176,768]{1,0:T(8,128)(2,1)S(1)}, u32[]{:S(2)}) copy-start(bf16[176,768]{1,0:T(8,128)(2,1)S(1)} %collective-permute-done.10.e2_ref) | copy-start | bytes 811012
  97.5 1.6 %collective-permute-start.12 = (bf16[176,768]{1,0:T(8,128)(2,1)S(1)}, bf16[176,768]{1,0:T(8,128)(2,1)S(1)}, u32[]{:S(2)}, u32[]{:S(2)}) collective-permute-start(bf16[176,768]{1,0:T(8,128)(2,1)S(1)} %collective-permute-done.10.e2_ref), channel_id=1, source_target_pairs={{0,1},{1,0},{2,3},{3,2},{4,5},{5,4},{6,7},{7,6},{8,9},{9,8},{10,11... | collective-permute-start | bytes 811016 | tf_op jit(solution)/shard_map/ppermute | solution.py:27
  97.9 1.3 copy-start.7
  99.1 0.7 copy-start.8
  112.9 39.7 %all-to-all-start.2 = ((bf16[8,88,2048]{2,1,0:T(8,128)(2,1)}), bf16[8,88,2048]{2,1,0:T(8,128)(2,1)S(1)}, u32[]{:S(2)}, u32[]{:S(2)}) async-start(bf16[8,88,2048]{2,1,0:T(8,128)(2,1)} %bitcast.11), calls=%async_computation.3 | async-start | bytes 5767168 | tf_op jit(solution)/shard_map/all_to_all | solution.py:326
  152.6 1.0 copy-start.3
Sparse Core Ops, SparseCore 0:
  113.0 38.5 reduce-scatter.1

commit v2 on v0

v2 whole, which is shorter than its diff:
```python
import functools

import jax
import jax.numpy as jnp
from jax import lax
from jax.experimental import pallas as pl
from jax.experimental.pallas import tpu as pltpu
from jax.sharding import Mesh, PartitionSpec as P

F32 = jnp.float32
BF16 = jnp.bfloat16
NEG = 7
ROWS = 88
PADDED = 96
FEAT = 1024
TOTAL = 8 * ROWS
QUARTER = 2 * ROWS
WIDE = 768
LAST = 640
SCALE = 4096 ** (-0.5)
MIB = 1024 * 1024
NT = (((1,), (1,)), ((), ()))
NN = (((1,), (0,)), ((), ()))
TN = (((0,), (0,)), ((), ()))
HBM = pl.BlockSpec(memory_space=pltpu.HBM)
VMEM = pl.BlockSpec(memory_space=pltpu.VMEM)
PIECES = ((0, 0), (1, 0), (2, 0), (3, 0), (4, 0), (4, 48), (5, 0), (6, 0), (7, 0))


def shift(x, axis, count, step):
    return lax.ppermute(x, axis, [(i, (i + step) % count) for i in range(count)])


def gather_z(x):
    half = PADDED // 2
    r1 = shift(x, "z", 8, 1)
    l1 = shift(x, "z", 8, -1)
    r2 = shift(r1, "z", 8, 1)
    l2 = shift(l1, "z", 8, -1)
    r3 = shift(r2, "z", 8, 1)
    l3 = shift(l2, "z", 8, -1)
    r4 = shift(r3[:half], "z", 8, 1)
    l4 = shift(l3[half:], "z", 8, -1)
    return [x, r1, r2, r3, r4, l4, l3, l2, l1]


def position(*axes):
    return tuple(lax.axis_index(a) for a in axes)


def dot(a, b, dims):
    return lax.dot_general(a, b, dims, preferred_element_type=F32)


def in_block(column, b):
    return (column >= b * ROWS) & (column < b * ROWS + ROWS)


def pad_rows(x):
    return jnp.concatenate([x, jnp.zeros((PADDED - ROWS, x.shape[1]), x.dtype)])


def prepare_kernel(q_ref, p_ref, n_ref, owner_ref, row_ref, q_out_ref, out_ref, turn_ref):
    for b in range(8):
        out_ref[b, :, :FEAT] = p_ref[...]
        out_ref[b, :, FEAT:] = n_ref[...]
    q_out_ref[:, :FEAT] = pad_rows(q_ref[...].astype(F32)).astype(BF16)
    lane = lax.broadcasted_iota(jnp.int32, (PADDED, 128), 1).astype(F32)
    turn_ref[...] = jnp.zeros((128, 128), F32)
    turn_ref[:NEG, :ROWS] = owner_ref[...].astype(F32)
    turn_ref[8 : 8 + NEG, :ROWS] = row_ref[...].astype(F32)
    turned = jnp.transpose(turn_ref[...])[:PADDED]
    named = jnp.full((PADDED, 128), -1.0, F32)
    for k in range(NEG):
        named = jnp.where(lane == turned[:, k : k + 1], turned[:, 8 + k : 9 + k], named)
    q_out_ref[:, FEAT:] = named.astype(BF16)


def join_kernel(*refs):
    z = lax.axis_index("z")
    for ref, (k, first) in zip(refs[:9], PIECES):
        row = pl.multiple_of(lax.rem(z + 8 - k, 8) * PADDED + first, 16)
        refs[9][pl.ds(row, ref.shape[0]), :] = ref[...]


def mask_parts(z):
    owner = lax.broadcasted_iota(jnp.int32, (128, TOTAL), 0)
    column = lax.broadcasted_iota(jnp.int32, (128, TOTAL), 1)
    here = (owner < 64) & (((owner >> 1) & 7) == z)
    spot = (owner >> 4) * 2 + (owner & 1)
    spread = jnp.where(here & in_block(column, spot), 1.0, 0.0).astype(BF16)
    inner = column[:8]
    for b in range(1, 8):
        inner = inner - jnp.where(column[:8] >= b * ROWS, ROWS, 0)
    return spread, inner[:1].astype(F32), here, spot


def score_kernel(give, q_ref, pn_ref, out_ref):
    z, xh, core = position("z", "xh", "c")
    half = 1 - core if give else core
    mine = pl.ds(pl.multiple_of(half * 4 * PADDED, 4 * PADDED), 4 * PADDED)
    q, names = q_ref[mine, :FEAT], q_ref[mine, FEAT:]
    spread, inner, here, spot = mask_parts(z)
    mask = dot(names, spread, NN) == inner
    named = jnp.where(mask, dot(q, pn_ref[:, FEAT:], NT), 0.0)
    row = lax.broadcasted_iota(jnp.int32, (TOTAL, 128), 0)
    lane = lax.broadcasted_iota(jnp.int32, (TOTAL, 128), 1)
    gather = jnp.where((lane < 16) & in_block(row, lane & 7), 1.0, 0.0)
    value = lax.dot_general(
        named, gather, NN, precision=lax.Precision.HIGHEST, preferred_element_type=F32
    )
    lane_b = lax.broadcasted_iota(jnp.int32, (128, 128), 1)
    pick = here[:, :128] & (spot[:, :128] == (lane_b & 7)) & (lane_b < 16)
    at_block = dot(names, jnp.where(pick, 1.0, 0.0).astype(BF16), NN)
    tail = jnp.where((at_block >= 0.0) & (lane[: 4 * PADDED] < 16), value, -jnp.inf)
    scores = dot(q, pn_ref[:, :FEAT], NT)
    for t in range(4):
        slot = pl.ds(jnp.where(xh == t // 2, 0, 1), 1)
        rows = slice(t % 2 * ROWS, (t % 2 + 1) * ROWS)
        here_t = slice(t * PADDED, t * PADDED + ROWS)
        out_ref[slot, rows, :TOTAL] = scores[None, here_t]
        out_ref[slot, rows, TOTAL:] = tail[None, here_t, : WIDE - TOTAL]


def soft_kernel(keep_ref, near_ref, far_ref, e_ref, stats_ref, turn_ref):
    y, z, xl, xh, core = position("y", "z", "xl", "xh", "c")
    stats_ref[...] = jnp.zeros(stats_ref.shape, F32)
    column = lax.broadcasted_iota(jnp.int32, (ROWS, WIDE), 1)
    row = lax.broadcasted_iota(jnp.int32, (ROWS, WIDE), 0)
    once = column < TOTAL + 8
    diagonal = column == row + (y * 2 + xl) * ROWS
    lane = lax.broadcasted_iota(jnp.int32, (ROWS, 128), 1)
    for h in range(2):
        rows = slice(h * ROWS, (h + 1) * ROWS)
        scores = (keep_ref[0, rows, :] + near_ref[0, rows, :] + far_ref[0, rows, :]) * SCALE
        peak = jnp.max(scores, axis=1, keepdims=True)
        e = jnp.exp(scores - peak)
        e_ref[rows, :] = e
        part = jnp.sum(jnp.where(once, e, 0.0), axis=1, keepdims=True)
        own = diagonal & (core * 4 + xh * 2 + h == z)
        positive = jnp.sum(jnp.where(own, scores, 0.0), axis=1, keepdims=True)
        info = jnp.where(lane == 0, peak, jnp.where(lane == 1, part, positive))
        turn_ref[...] = jnp.zeros((128, 128), F32)
        turn_ref[:ROWS, :] = info
        turned = jnp.transpose(turn_ref[...])
        for v in range(3):
            at = 2 * v + h
            stats_ref[:, at : at + 1, :] = jnp.broadcast_to(turned[None, v : v + 1], (8, 1, 128))


def settle_kernel(stats_ref, e_ref, out_ref, turn_ref):
    y, z, xl, xh, core = position("y", "z", "xl", "xh", "c")
    every = stats_ref[...]
    own = stats_ref[pl.ds(z, 1)][0]
    top = jnp.max(every[:, 0:2, :], axis=0)
    whole = jnp.sum(every[:, 2:4, :] * jnp.exp(every[:, 0:2, :] - top[None]), axis=0)
    log_total = top + jnp.log(whole)
    valid = lax.broadcasted_iota(jnp.int32, (2, 128), 1) < ROWS
    loss = log_total - own[4:6]
    turn_ref[...] = jnp.zeros((128, 128), F32)
    turn_ref[0:2, :] = jnp.where(valid, jnp.exp(own[0:2] - log_total), 0.0)
    turn_ref[2:4, :] = jnp.where(valid, loss, 0.0)
    turned = jnp.transpose(turn_ref[...])[:ROWS]
    column = lax.broadcasted_iota(jnp.int32, (ROWS, WIDE), 1)
    row = lax.broadcasted_iota(jnp.int32, (ROWS, WIDE), 0)
    diagonal = column == row + (y * 2 + xl) * ROWS
    parts = []
    for h in range(2):
        weight = e_ref[h * ROWS : (h + 1) * ROWS, :] * turned[:, h : h + 1]
        loss_h = turned[:, 2 + h : 3 + h]
        mine = diagonal & (core * 4 + xh * 2 + h == z)
        weight = jnp.where(mine, 0.0, weight)
        high = weight.astype(BF16).astype(F32)
        weight = jnp.where(column < TOTAL + 8, high, weight - high)
        loss_a = loss_h.astype(BF16).astype(F32)
        loss_b = (loss_h - loss_a).astype(BF16).astype(F32)
        weight = jnp.where(column == TOTAL + 16, loss_a, weight)
        weight = jnp.where(column == TOTAL + 17, loss_b, weight)
        weight = jnp.where(column == TOTAL + 18, loss_h - loss_a - loss_b, weight)
        parts.append(pad_rows(weight))
    out_ref[...] = jnp.concatenate(parts).astype(BF16)


def weight_kernel(
    e0_ref, e1_ref, e2_ref, e3_ref, pn_ref, q_ref,
    out_ref, gq_ref, loss_ref, diagonal_ref, w_ref, named_ref, turn_ref,
):
    y, z, xl, xh, core = position("y", "z", "xl", "xh", "c")
    lane = lax.broadcasted_iota(jnp.int32, (128, TOTAL), 0) - (TOTAL - LAST)
    wide = lax.broadcasted_iota(jnp.int32, (128, TOTAL), 1)
    spread = (lane >= 0) & (lane < 8) & in_block(wide, lane)
    spread = jnp.where(spread, 1.0, 0.0).astype(BF16)
    names, inner, _, _ = mask_parts(z)
    turn_ref[...] = jnp.zeros((128, 128), F32)

    def body(e_ref, quarter):
        rows = slice(quarter * 2 * PADDED, (quarter + 1) * 2 * PADDED)
        w_ref[rows, :] = e_ref[:, :TOTAL]
        mask = dot(q_ref[rows, FEAT:], names, NN) == inner
        value = dot(e_ref[:, LAST:], spread, NN)
        named_ref[rows, :] = jnp.where(mask, value, 0.0).astype(BF16)
        for h in range(2):

            @pl.when(z == 2 * quarter + h)
            def _(h=h):
                turn_ref[:PADDED, :] = e_ref[h * PADDED : (h + 1) * PADDED, LAST:].astype(F32)

    parts = ((e0_ref, 0, 0), (e1_ref, 1, 0), (e2_ref, 0, 1), (e3_ref, 1, 1))
    for e_ref, a, b in parts:
        for quarter in range(4):
            here = (core == (quarter // 2 ^ a)) & (xh == (quarter % 2 ^ b))
            pl.when(here)(functools.partial(body, e_ref, quarter))

    gq = dot(w_ref[...], pn_ref[:, :FEAT], NN) + dot(named_ref[...], pn_ref[:, FEAT:], NN)
    gq = SCALE * gq
    for b in range(8):
        gq_ref[b] = gq[b * PADDED : b * PADDED + ROWS].astype(BF16)
    first = TOTAL + 16 - LAST
    loss = jnp.sum(turn_ref[:PADDED, first : first + 3], axis=1, keepdims=True)
    weight = jnp.exp(-loss) - 1.0
    diagonal_ref[...] = jnp.broadcast_to(weight, (PADDED, 128))
    own = pl.ds(pl.multiple_of(z * PADDED, 16), PADDED)
    column = lax.broadcasted_iota(jnp.int32, (PADDED, TOTAL), 1)
    row = lax.broadcasted_iota(jnp.int32, (PADDED, TOTAL), 0)
    here = (column == row + (y * 2 + xl) * ROWS) & (row < ROWS)
    w_ref[own, :] = jnp.where(here, weight, w_ref[own, :].astype(F32)).astype(BF16)
    q = q_ref[:, :FEAT]
    out_ref[:, :FEAT] = (SCALE * dot(w_ref[...], q, TN)).astype(BF16)
    out_ref[:, FEAT:] = (SCALE * dot(named_ref[...], q, TN)).astype(BF16)
    turned = jnp.transpose(turn_ref[...])
    loss = turned[first : first + 1] + turned[first + 1 : first + 2] + turned[first + 2 : first + 3]
    loss_ref[...] = jnp.broadcast_to(loss, (8, 128))


def finish_kernel(gq_ref, diagonal_ref, p_ref, x_ref, gq_out_ref, gp_out_ref, gn_out_ref):
    own = SCALE * diagonal_ref[:ROWS, :1] * p_ref[...].astype(F32)
    gq_out_ref[...] = (gq_ref[...].astype(F32) + own).astype(BF16)
    for first, out_ref in ((0, gp_out_ref), (FEAT, gn_out_ref)):
        total = x_ref[0, :, first : first + FEAT].astype(F32)
        for b in range(1, 8):
            total += x_ref[b, :, first : first + FEAT].astype(F32)
        out_ref[...] = total.astype(BF16)


def shaped(shape, dtype):
    return jax.ShapeDtypeStruct(shape, dtype)


def block(shape):
    return pl.BlockSpec(shape, lambda i: (0,) * len(shape))


def call(kernel, name, operands, outs, scratch=(), far_in=0, far_out=(), limit=20):
    return pl.pallas_call(
        kernel,
        out_shape=outs,
        in_specs=[VMEM] * (len(operands) - far_in) + [HBM] * far_in,
        out_specs=tuple(HBM if i in far_out else VMEM for i in range(len(outs))),
        scratch_shapes=scratch,
        compiler_params=pltpu.CompilerParams(vmem_limit_bytes=limit * MIB),
        cost_estimate=pl.CostEstimate(flops=0, bytes_accessed=1024, transcendentals=0),
        name=name,
    )(*operands)


def blocked(kernel, name, operands, in_specs, outs, scratch=(), limit=60):
    return pl.pallas_call(
        kernel,
        out_shape=outs,
        grid=(1,),
        in_specs=in_specs,
        out_specs=tuple(block(s.shape) for s in outs),
        scratch_shapes=scratch,
        compiler_params=pltpu.CompilerParams(vmem_limit_bytes=limit * MIB),
        name=name,
    )(*operands)


def local(queries, passages, negatives, neg_owner, neg_row):
    plane = ("y", "xl")
    packed, spread = blocked(
        prepare_kernel, "prepare", (queries, passages, negatives, neg_owner.T, neg_row.T),
        [block((ROWS, FEAT))] * 3 + [block((NEG, ROWS))] * 2,
        (shaped((PADDED, FEAT + 128), BF16), shaped((8, ROWS, 2 * FEAT), BF16)),
        scratch=[pltpu.VMEM((128, 128), F32)],
    )
    pn = lax.all_to_all(spread, plane, 0, 0, tiled=True).reshape(TOTAL, 2 * FEAT)
    pieces = gather_z(packed)

    q_cat = call(join_kernel, "join", pieces, (shaped((8 * PADDED, FEAT + 128), BF16),))[0]

    def scores_half(give):
        return call(
            functools.partial(score_kernel, give), "scores_give" if give else "scores_keep",
            (q_cat, pn), (shaped((2, QUARTER, WIDE), F32),),
        )[0]

    give = scores_half(True)
    near = shift(give, "c", 2, 1)
    keep = scores_half(False)
    far = shift(keep[1:] + near[1:], "xh", 2, 1)

    e, stats = call(
        soft_kernel, "soft", (keep, near, far),
        (shaped((QUARTER, WIDE), F32), shaped((8, 8, 128), F32)), [pltpu.VMEM((128, 128), F32)],
    )
    stats = lax.all_to_all(stats, "z", 0, 0, tiled=True)
    e0 = call(
        settle_kernel, "settle", (stats, e), (shaped((2 * PADDED, WIDE), BF16),),
        [pltpu.VMEM((128, 128), F32)],
    )[0]
    e2 = shift(e0, "xh", 2, 1)
    e1 = shift(e0, "c", 2, 1)
    e3 = shift(e2, "c", 2, 1)

    gpn, gq, loss, diagonal = call(
        weight_kernel, "weights", (e0, e1, e2, e3, pn, q_cat),
        (
            shaped((TOTAL, 2 * FEAT), BF16), shaped((8, ROWS, FEAT), BF16),
            shaped((8, 128), F32), shaped((PADDED, 128), F32),
        ),
        [pltpu.VMEM((8 * PADDED, TOTAL), BF16)] * 2 + [pltpu.VMEM((128, 128), F32)],
        limit=24,
    )
    grad_queries = lax.psum_scatter(gq, "z", scatter_dimension=0, tiled=True)[0]
    gpn = lax.all_to_all(gpn.reshape(8, ROWS, 2 * FEAT), plane, 0, 0, tiled=True)
    grads = blocked(
        finish_kernel, "finish", (grad_queries, diagonal, passages, gpn),
        [block((ROWS, FEAT)), block((PADDED, 128)), block((ROWS, FEAT)), VMEM],
        (shaped((ROWS, FEAT), BF16),) * 3, limit=20,
    )
    return (loss[0, :ROWS],) + tuple(grads)


def solution(mesh):
    fine = Mesh(mesh.devices.reshape(4, 8, 2, 2, 2), ("y", "z", "xl", "xh", "c"))
    dp, width = ("y", "z", "xl"), ("xh", "c")
    in_specs = (P(dp, width), P(dp, width), P(dp, width), P(dp, None), P(dp, None))
    out_specs = (P(dp), P(dp, width), P(dp, width), P(dp, width))
    return jax.shard_map(local, mesh=fine, in_specs=in_specs, out_specs=out_specs, check_vma=False)
```

time: 824 us -> 161 us (0.20)
  waiting for transfers between devices: 555 us -> 73.7 us
  local copies, waits for them, and re-layouts: 138 us -> 6.86 us
  other arithmetic: 29.7 us -> 0.06 us
  matrix products: 24.1 us -> 0 us
  blocking collectives: 33.2 us -> 15.7 us
  Pallas kernels: 0 us -> 17.1 us
    all_gather x2 -> x0, waiting for transfers between devices: 500 us -> none  [the longest x1 327 us: local(): every_passage = lax.all_gather(passages, 'dp', axis=0, tiled=True)]
    scatter x3 -> x0, local copies, waits for them, and re-layouts: 98 us -> none  [the longest x2 65.2 us: local(): outgoing = jnp.zeros((dev_count, capacity, feature_count), jnp.bfloat16)....]
    ppermute x0 -> x13, waiting for transfers between devices: none -> 38.3 us  [shift(): lax.ppermute(x, axis, [(i, (i + step) % count) for i in range(count)])]
    dot_general x4 -> x0, matrix products: 24.1 us -> none  [the longest x1 9.28 us: local(): jnp.einsum('qd,pd->qp', queries, every_passage, preferred_element_type=jn...]
    ppermute x0 -> x13, starting transfers between devices: none -> 23.1 us  [shift(): lax.ppermute(x, axis, [(i, (i + step) % count) for i in range(count)])]
    gather x3 -> x0, local copies, waits for them, and re-layouts: 18.7 us -> none  [the longest x1 11.8 us: local(): fetched[owner_flat, slot_index].reshape(row_count, neg_count, feature_count)]
    all_to_all x3 -> x2, waiting for transfers between devices: 53.3 us -> 35.4 us  [the longest x1 35.4 us: local(): lax.all_to_all(gpn.reshape(8, ROWS, 2 * FEAT), plane, 0, 0, tiled=True)]
    all_to_all x3 -> x2, starting transfers between devices: 25.5 us -> 7.58 us  [the longest x1 3.79 us: local(): lax.all_to_all(spread, plane, 0, 0, tiled=True).reshape(TOTAL, 2 * FEAT)]
  transfers between devices with their start and end apart: 6 -> 16, of which waited for: 3 -> 9; matrix products, arithmetic and copies ran while one was open for 19% -> 0% of each run, Pallas kernels for 0% -> 2%
where the time goes in v2:
time: 161 us; the launch traced here: 158 us
  waiting for transfers between devices  73.7 us (46%)
  starting transfers between devices  30.7 us (19%)
  Pallas kernels  17.1 us (11%)
  blocking collectives  15.7 us (10%)
  between operations  14.2 us (9%)
  local copies, waits for them, and re-layouts  6.86 us (4%)
    ppermute x13, waiting for transfers between devices, shift(): lax.ppermute(x, axis, [(i, (i + step) % count) for i in range(count)])  38.3 us
    all_to_all x1, waiting for transfers between devices, local(): lax.all_to_all(gpn.reshape(8, ROWS, 2 * FEAT), plane, 0, 0, tiled=True)  35.4 us
    ppermute x13, starting transfers between devices, shift(): lax.ppermute(x, axis, [(i, (i + step) % count) for i in range(count)])  23.1 us
    all_to_all x1, blocking collectives, local(): stats = lax.all_to_all(stats, 'z', 0, 0, tiled=True)  15.7 us
    pallas_call x6, Pallas kernels, call(): pl.pallas_call(kernel, out_shape=outs, in_specs=[VMEM] * (len(operands) -...  12.6 us
    unnamed x16, local copies, waits for them, and re-layouts  6.33 us
    pallas_call x2, Pallas kernels, blocked(): pl.pallas_call(kernel, out_shape=outs, grid=(1,), in_specs=in_specs, out_...  4.49 us
    all_to_all x1, starting transfers between devices, local(): lax.all_to_all(spread, plane, 0, 0, tiled=True).reshape(TOTAL, 2 * FEAT)  3.79 us
  transfers between devices with their start and end apart: 16, of which 9 were waited for; matrix products, arithmetic and copies ran while one was open for 0% of the time, Pallas kernels for 2%

profile of v2, /device:TPU:0, one launch (start us, length us, event | category | flops | bytes accessed | tf_op | source)
XLA Modules:
  0.0 158.3 jit_solution(17435092068367050514)
XLA Ops:
  7.2 3.2 %prepare.1 = (bf16[96,1152]{1,0:T(8,128)(2,1)}, bf16[8,88,2048]{2,1,0:T(8,128)(2,1)}) custom-call(bf16[88,1024]{1,0:T(8,128)(2,1)} %q_ref.1, bf16[88,1024]{1,0:T(8,128)(2,1)} %p_ref.3, bf16[88,1024]{1,0:T(8,128)(2,1)} %n_ref.1, s32[7,88]{1,0:T(8,128)} %bitcast.12, s32[7,88]{1,0:T(8,128)} %bitcast.13), custom_call_target="tpu_custom_call" | custom-call | tf_op jit(solution)/shard_map/prepare/pallas_call | solution.py:267
  10.4 0.0 copy-start.6
  10.4 3.8 %all-to-all-start = ((bf16[8,88,2048]{2,1,0:T(8,128)(2,1)}), bf16[8,88,2048]{2,1,0:T(8,128)(2,1)S(1)}, u32[]{:S(2)}, u32[]{:S(2)}) async-start(bf16[8,88,2048]{2,1,0:T(8,128)(2,1)} %get-tuple-element.16), calls=%async_computation | async-start | bytes 5767168 | tf_op jit(solution)/shard_map/all_to_all | solution.py:287
  14.1 0.0 reduce-scatter.2.cloned.1.call-start
  14.2 0.0 copy-done.6
  14.2 5.9 %collective-permute-start.4 = (bf16[96,1152]{1,0:T(8,128)(2,1)S(1)}, bf16[96,1152]{1,0:T(8,128)(2,1)S(1)}, u32[]{:S(2)}, u32[]{:S(2)}) collective-permute-start(bf16[96,1152]{1,0:T(8,128)(2,1)S(1)} %copy-done.6), channel_id=1, source_target_pairs={{0,56},{8,0},{16,8},{24,16},{32,24},{40,32},{48,40},{56,48},{1,57}... | collective-permute-start | bytes 663560 | tf_op jit(solution)/shard_map/ppermute | solution.py:31
  20.1 0.0 collective-permute-start
  20.1 4.4 %collective-permute-done.4.refs_8_ = bf16[96,1152]{1,0:T(8,128)(2,1)S(1)} collective-permute-done((bf16[96,1152]{1,0:T(8,128)(2,1)S(1)}, bf16[96,1152]{1,0:T(8,128)(2,1)S(1)}, u32[]{:S(2)}, u32[]{:S(2)}) %collective-permute-start.4) | collective-permute-done | bytes 221216 | tf_op jit(solution)/shard_map/ppermute | solution.py:31
  24.5 3.7 %collective-permute-start.5 = (bf16[96,1152]{1,0:T(8,128)(2,1)S(1)}, bf16[96,1152]{1,0:T(8,128)(2,1)S(1)}, u32[]{:S(2)}, u32[]{:S(2)}) collective-permute-start(bf16[96,1152]{1,0:T(8,128)(2,1)S(1)} %collective-permute-done.4.refs_8_), channel_id=1, source_target_pairs={{0,56},{8,0},{16,8},{24,16},{32,24},{40,32},{48,40},{56,48},{1,57}... | collective-permute-start | bytes 663560 | tf_op jit(solution)/shard_map/ppermute | solution.py:31
  28.2 0.0 collective-permute-done.refs_1_
  28.2 0.0 collective-permute-start.1
  28.2 3.5 %collective-permute-done.5.refs_7_ = bf16[96,1152]{1,0:T(8,128)(2,1)S(1)} collective-permute-done((bf16[96,1152]{1,0:T(8,128)(2,1)S(1)}, bf16[96,1152]{1,0:T(8,128)(2,1)S(1)}, u32[]{:S(2)}, u32[]{:S(2)}) %collective-permute-start.5) | collective-permute-done | bytes 221216 | tf_op jit(solution)/shard_map/ppermute | solution.py:31
  31.7 3.7 %collective-permute-start.6 = (bf16[96,1152]{1,0:T(8,128)(2,1)S(1)}, bf16[96,1152]{1,0:T(8,128)(2,1)S(1)}, u32[]{:S(2)}, u32[]{:S(2)}) collective-permute-start(bf16[96,1152]{1,0:T(8,128)(2,1)S(1)} %collective-permute-done.5.refs_7_), channel_id=1, source_target_pairs={{0,56},{8,0},{16,8},{24,16},{32,24},{40,32},{48,40},{56,48},{1,57}... | collective-permute-start | bytes 663560 | tf_op jit(solution)/shard_map/ppermute | solution.py:31
  35.4 0.0 collective-permute-done.1.refs_2_
  35.4 0.0 collective-permute-start.2
  35.4 3.4 %collective-permute-done.6.refs_6_ = bf16[96,1152]{1,0:T(8,128)(2,1)S(1)} collective-permute-done((bf16[96,1152]{1,0:T(8,128)(2,1)S(1)}, bf16[96,1152]{1,0:T(8,128)(2,1)S(1)}, u32[]{:S(2)}, u32[]{:S(2)}) %collective-permute-start.6) | collective-permute-done | bytes 221216 | tf_op jit(solution)/shard_map/ppermute | solution.py:31
  38.9 3.8 %collective-permute-start.7 = (bf16[48,1152]{1,0:T(8,128)(2,1)S(1)}, bf16[48,1152]{1,0:T(8,128)(2,1)S(1)}, u32[]{:S(2)}, u32[]{:S(2)}) collective-permute-start(bf16[48,1152]{1,0:T(8,128)(2,1)S(1)} %slice.21), channel_id=1, source_target_pairs={{0,56},{8,0},{16,8},{24,16},{32,24},{40,32},{48,40},{56,48},{1,57}... | collective-permute-start | bytes 331784 | tf_op jit(solution)/shard_map/ppermute | solution.py:31
  42.7 0.0 collective-permute-done.2.refs_3_
  42.7 0.1 collective-permute-start.3
  42.8 2.2 %collective-permute-done.7.refs_5_ = bf16[48,1152]{1,0:T(8,128)(2,1)S(1)} collective-permute-done((bf16[48,1152]{1,0:T(8,128)(2,1)S(1)}, bf16[48,1152]{1,0:T(8,128)(2,1)S(1)}, u32[]{:S(2)}, u32[]{:S(2)}) %collective-permute-start.7) | collective-permute-done | bytes 110624 | tf_op jit(solution)/shard_map/ppermute | solution.py:31
  45.0 3.7 %collective-permute-done.3.refs_4_ = bf16[48,1152]{1,0:T(8,128)(2,1)S(1)} collective-permute-done((bf16[48,1152]{1,0:T(8,128)(2,1)S(1)}, bf16[48,1152]{1,0:T(8,128)(2,1)S(1)}, u32[]{:S(2)}, u32[]{:S(2)}) %collective-permute-start.3) | collective-permute-done | bytes 110624 | tf_op jit(solution)/shard_map/ppermute | solution.py:31
  48.7 0.1 join.1.q_ref
  48.9 0.0 copy-start
  48.9 1.2 copy-done
  50.1 0.0 all-to-all-done
  50.1 0.0 copy-start.1
  50.1 1.5 copy-done.1
  51.6 2.7 %scores_give.1 = f32[2,176,768]{2,1,0:T(8,128)S(1)} custom-call(bf16[768,1152]{1,0:T(8,128)(2,1)S(1)} %copy-done.1, bf16[704,2048]{1,0:T(8,128)(2,1)S(1)} %bitcast.7), custom_call_target="tpu_custom_call" | custom-call | bytes 1024 | tf_op jit(solution)/shard_map/scores_give/pallas_call | solution.py:254
  54.3 0.3 collective-permute-start.8
  54.6 2.7 %scores_keep.1.keep_ref = f32[2,176,768]{2,1,0:T(8,128)S(1)} custom-call(bf16[768,1152]{1,0:T(8,128)(2,1)S(1)} %copy-done.1, bf16[704,2048]{1,0:T(8,128)(2,1)S(1)} %bitcast.8), custom_call_target="tpu_custom_call" | custom-call | bytes 1024 | tf_op jit(solution)/shard_map/scores_keep/pallas_call | solution.py:254
  57.2 0.0 collective-permute-done.8.near_ref
  57.3 0.1 slice_add_fusion
  57.3 0.0 copy-start.2
  57.3 2.8 %collective-permute-start.9 = (f32[1,176,768]{2,1,0:T(8,128)S(1)}, f32[1,176,768]{2,1,0:T(8,128)S(1)}, u32[]{:S(2)}, u32[]{:S(2)}) collective-permute-start(f32[1,176,768]{2,1,0:T(8,128)S(1)} %slice_add_fusion), channel_id=1, source_target_pairs={{0,2},{2,0},{1,3},{3,1},{4,6},{6,4},{5,7},{7,5},{8,10},{10,8},{9,1... | collective-permute-start | bytes 1622024 | tf_op jit(solution)/shard_map/ppermute | solution.py:31
  60.1 13.5 %collective-permute-done.9.far_ref = f32[1,176,768]{2,1,0:T(8,128)S(1)} collective-permute-done((f32[1,176,768]{2,1,0:T(8,128)S(1)}, f32[1,176,768]{2,1,0:T(8,128)S(1)}, u32[]{:S(2)}, u32[]{:S(2)}) %collective-permute-start.9) | collective-permute-done | bytes 540704 | tf_op jit(solution)/shard_map/ppermute | solution.py:31
  73.6 0.4 soft.1
  74.0 15.7 %all_to_all.15.stats_ref = f32[8,8,128]{2,1,0:T(8,128)S(1)} all-to-all(f32[8,8,128]{2,1,0:T(8,128)S(1)} %get-tuple-element.17), channel_id=1, replica_groups=mesh['y'=4,'z'=8,'xl'=2,'xh'=2,'c'=2] {'z'}, dimensions={0} | all-to-all | bytes 65536 | tf_op jit(solution)/shard_map/all_to_all | solution.py:307
  89.7 0.3 settle.1.e0_ref
  90.0 2.8 %collective-permute-start.11 = (bf16[192,768]{1,0:T(8,128)(2,1)S(1)}, bf16[192,768]{1,0:T(8,128)(2,1)S(1)}, u32[]{:S(2)}, u32[]{:S(2)}) collective-permute-start(bf16[192,768]{1,0:T(8,128)(2,1)S(1)} %settle.1.e0_ref), channel_id=1, source_target_pairs={{0,2},{2,0},{1,3},{3,1},{4,6},{6,4},{5,7},{7,5},{8,10},{10,8},{9,1... | collective-permute-start | bytes 884744 | tf_op jit(solution)/shard_map/ppermute | solution.py:31
  92.8 0.0 collective-permute-start.10
  92.8 6.0 %collective-permute-done.11.e2_ref = bf16[192,768]{1,0:T(8,128)(2,1)S(1)} collective-permute-done((bf16[192,768]{1,0:T(8,128)(2,1)S(1)}, bf16[192,768]{1,0:T(8,128)(2,1)S(1)}, u32[]{:S(2)}, u32[]{:S(2)}) %collective-permute-start.11) | collective-permute-done | bytes 294944 | tf_op jit(solution)/shard_map/ppermute | solution.py:31
  98.8 0.0 collective-permute-start.12
  98.8 0.0 collective-permute-done.10.e1_ref
  98.8 1.6 collective-permute-done.12.e3_ref
  100.4 0.0 copy-done.2
  100.4 6.4 %weights.1 = (bf16[704,2048]{1,0:T(8,128)(2,1)S(1)}, bf16[8,88,1024]{2,1,0:T(8,128)(2,1)S(1)}, f32[8,128]{1,0:T(8,128)S(1)}, f32[96,128]{1,0:T(8,128)S(1)}) custom-call(bf16[192,768]{1,0:T(8,128)(2,1)S(1)} %settle.1.e0_ref, bf16[192,768]{1,0:T(8,128)(2,1)S(1)} %collective-permute-done.10.e1_ref, bf16[192,768]{1,0:T(8,128)(2,1)S(1)} %collective-permute-done.11.e2_ref, ...), custom_call_target="tpu_custom_call" | custom-call | bytes 1024 | tf_op jit(solution)/shard_map/weights/pallas_call | solution.py:254
  106.8 0.0 copy-start.3
  106.8 1.5 copy-done.3
  108.4 0.0 copy-start.4
  108.4 1.1 copy-done.4
  109.5 0.0 reduce-scatter.2.cloned.1.call-update
  109.5 0.0 copy-start.5
  109.5 3.8 %all-to-all-start.2 = ((bf16[8,88,2048]{2,1,0:T(8,128)(2,1)}), bf16[8,88,2048]{2,1,0:T(8,128)(2,1)S(1)}, u32[]{:S(2)}, u32[]{:S(2)}) async-start(bf16[8,88,2048]{2,1,0:T(8,128)(2,1)} %bitcast.10), calls=%async_computation.3 | async-start | bytes 5767168 | tf_op jit(solution)/shard_map/all_to_all | solution.py:326
  113.3 0.5 slice_bitcast_fusion
  113.8 35.4 %all-to-all-done.2.x_ref = bf16[8,88,2048]{2,1,0:T(8,128)(2,1)S(1)} async-done(((bf16[8,88,2048]{2,1,0:T(8,128)(2,1)}), bf16[8,88,2048]{2,1,0:T(8,128)(2,1)S(1)}, u32[]{:S(2)}, u32[]{:S(2)}) %all-to-all-start.2) | async-done | bytes 2883616 | tf_op jit(solution)/shard_map/all_to_all | solution.py:326
  149.2 0.0 reduce-scatter.2.cloned.1.call-done
  149.2 0.0 copy-done.5
  149.2 0.0 copy-start.7
  149.2 0.9 copy-done.7
  150.2 1.3 finish.1
  (2 shorter events, 0.0 us)
Async XLA Ops:
  10.4 3.8 %copy-start.6 = (bf16[96,1152]{1,0:T(8,128)(2,1)S(1)}, bf16[96,1152]{1,0:T(8,128)(2,1)}, u32[]{:S(2)}) copy-start(bf16[96,1152]{1,0:T(8,128)(2,1)} %get-tuple-element.15.refs_0_) | copy-start | bytes 663556
  10.4 39.8 %all-to-all-start = ((bf16[8,88,2048]{2,1,0:T(8,128)(2,1)}), bf16[8,88,2048]{2,1,0:T(8,128)(2,1)S(1)}, u32[]{:S(2)}, u32[]{:S(2)}) async-start(bf16[8,88,2048]{2,1,0:T(8,128)(2,1)} %get-tuple-element.16), calls=%async_computation | async-start | bytes 5767168 | tf_op jit(solution)/shard_map/all_to_all | solution.py:287
  14.1 135.1 %reduce-scatter.2.cloned.1.call-start = ((), (), s32[]{:S(2)}) async-start(), calls=%async_computation.4 | async-start | bytes 1622016 | tf_op jit(solution)/shard_map/reduce_scatter | solution.py:325
  14.2 10.3 %collective-permute-start.4 = (bf16[96,1152]{1,0:T(8,128)(2,1)S(1)}, bf16[96,1152]{1,0:T(8,128)(2,1)S(1)}, u32[]{:S(2)}, u32[]{:S(2)}) collective-permute-start(bf16[96,1152]{1,0:T(8,128)(2,1)S(1)} %copy-done.6), channel_id=1, source_target_pairs={{0,56},{8,0},{16,8},{24,16},{32,24},{40,32},{48,40},{56,48},{1,57}... | collective-permute-start | bytes 663560 | tf_op jit(solution)/shard_map/ppermute | solution.py:31
  20.1 8.1 %collective-permute-start = (bf16[96,1152]{1,0:T(8,128)(2,1)S(1)}, bf16[96,1152]{1,0:T(8,128)(2,1)S(1)}, u32[]{:S(2)}, u32[]{:S(2)}) collective-permute-start(bf16[96,1152]{1,0:T(8,128)(2,1)S(1)} %copy-done.6), channel_id=1, source_target_pairs={{0,8},{8,16},{16,24},{24,32},{32,40},{40,48},{48,56},{56,0},{1,9},... | collective-permute-start | bytes 663560 | tf_op jit(solution)/shard_map/ppermute | solution.py:31
  24.5 7.2 %collective-permute-start.5 = (bf16[96,1152]{1,0:T(8,128)(2,1)S(1)}, bf16[96,1152]{1,0:T(8,128)(2,1)S(1)}, u32[]{:S(2)}, u32[]{:S(2)}) collective-permute-start(bf16[96,1152]{1,0:T(8,128)(2,1)S(1)} %collective-permute-done.4.refs_8_), channel_id=1, source_target_pairs={{0,56},{8,0},{16,8},{24,16},{32,24},{40,32},{48,40},{56,48},{1,57}... | collective-permute-start | bytes 663560 | tf_op jit(solution)/shard_map/ppermute | solution.py:31
  28.2 7.2 %collective-permute-start.1 = (bf16[96,1152]{1,0:T(8,128)(2,1)S(1)}, bf16[96,1152]{1,0:T(8,128)(2,1)S(1)}, u32[]{:S(2)}, u32[]{:S(2)}) collective-permute-start(bf16[96,1152]{1,0:T(8,128)(2,1)S(1)} %collective-permute-done.refs_1_), channel_id=1, source_target_pairs={{0,8},{8,16},{16,24},{24,32},{32,40},{40,48},{48,56},{56,0},{1,9},... | collective-permute-start | bytes 663560 | tf_op jit(solution)/shard_map/ppermute | solution.py:31
  31.7 7.1 %collective-permute-start.6 = (bf16[96,1152]{1,0:T(8,128)(2,1)S(1)}, bf16[96,1152]{1,0:T(8,128)(2,1)S(1)}, u32[]{:S(2)}, u32[]{:S(2)}) collective-permute-start(bf16[96,1152]{1,0:T(8,128)(2,1)S(1)} %collective-permute-done.5.refs_7_), channel_id=1, source_target_pairs={{0,56},{8,0},{16,8},{24,16},{32,24},{40,32},{48,40},{56,48},{1,57}... | collective-permute-start | bytes 663560 | tf_op jit(solution)/shard_map/ppermute | solution.py:31
  35.4 7.2 %collective-permute-start.2 = (bf16[96,1152]{1,0:T(8,128)(2,1)S(1)}, bf16[96,1152]{1,0:T(8,128)(2,1)S(1)}, u32[]{:S(2)}, u32[]{:S(2)}) collective-permute-start(bf16[96,1152]{1,0:T(8,128)(2,1)S(1)} %collective-permute-done.1.refs_2_), channel_id=1, source_target_pairs={{0,8},{8,16},{16,24},{24,32},{32,40},{40,48},{48,56},{56,0},{1,9},... | collective-permute-start | bytes 663560 | tf_op jit(solution)/shard_map/ppermute | solution.py:31
  38.9 6.1 %collective-permute-start.7 = (bf16[48,1152]{1,0:T(8,128)(2,1)S(1)}, bf16[48,1152]{1,0:T(8,128)(2,1)S(1)}, u32[]{:S(2)}, u32[]{:S(2)}) collective-permute-start(bf16[48,1152]{1,0:T(8,128)(2,1)S(1)} %slice.21), channel_id=1, source_target_pairs={{0,56},{8,0},{16,8},{24,16},{32,24},{40,32},{48,40},{56,48},{1,57}... | collective-permute-start | bytes 331784 | tf_op jit(solution)/shard_map/ppermute | solution.py:31
  42.7 6.0 %collective-permute-start.3 = (bf16[48,1152]{1,0:T(8,128)(2,1)S(1)}, bf16[48,1152]{1,0:T(8,128)(2,1)S(1)}, u32[]{:S(2)}, u32[]{:S(2)}) collective-permute-start(bf16[48,1152]{1,0:T(8,128)(2,1)S(1)} %slice.20), channel_id=1, source_target_pairs={{0,8},{8,16},{16,24},{24,32},{32,40},{40,48},{48,56},{56,0},{1,9},... | collective-permute-start | bytes 331784 | tf_op jit(solution)/shard_map/ppermute | solution.py:31
  48.9 1.3 copy-start
  50.1 1.5 copy-start.1
  54.3 3.0 %collective-permute-start.8 = (f32[2,176,768]{2,1,0:T(8,128)S(1)}, f32[2,176,768]{2,1,0:T(8,128)S(1)}, u32[]{:S(2)}, u32[]{:S(2)}) collective-permute-start(f32[2,176,768]{2,1,0:T(8,128)S(1)} %scores_give.1), channel_id=1, source_target_pairs={{0,1},{1,0},{2,3},{3,2},{4,5},{5,4},{6,7},{7,6},{8,9},{9,8},{10,11... | collective-permute-start | bytes 3244040 | tf_op jit(solution)/shard_map/ppermute | solution.py:31
  57.3 43.1 %copy-start.2 = (bf16[768,1152]{1,0:T(8,128)(2,1)S(1)}, bf16[768,1152]{1,0:T(8,128)(2,1)}, u32[]{:S(2)}) copy-start(bf16[768,1152]{1,0:T(8,128)(2,1)} %copy-done) | copy-start | bytes 5308420
  57.3 16.3 %collective-permute-start.9 = (f32[1,176,768]{2,1,0:T(8,128)S(1)}, f32[1,176,768]{2,1,0:T(8,128)S(1)}, u32[]{:S(2)}, u32[]{:S(2)}) collective-permute-start(f32[1,176,768]{2,1,0:T(8,128)S(1)} %slice_add_fusion), channel_id=1, source_target_pairs={{0,2},{2,0},{1,3},{3,1},{4,6},{6,4},{5,7},{7,5},{8,10},{10,8},{9,1... | collective-permute-start | bytes 1622024 | tf_op jit(solution)/shard_map/ppermute | solution.py:31
  90.0 8.8 %collective-permute-start.11 = (bf16[192,768]{1,0:T(8,128)(2,1)S(1)}, bf16[192,768]{1,0:T(8,128)(2,1)S(1)}, u32[]{:S(2)}, u32[]{:S(2)}) collective-permute-start(bf16[192,768]{1,0:T(8,128)(2,1)S(1)} %settle.1.e0_ref), channel_id=1, source_target_pairs={{0,2},{2,0},{1,3},{3,1},{4,6},{6,4},{5,7},{7,5},{8,10},{10,8},{9,1... | collective-permute-start | bytes 884744 | tf_op jit(solution)/shard_map/ppermute | solution.py:31
  92.8 6.0 %collective-permute-start.10 = (bf16[192,768]{1,0:T(8,128)(2,1)S(1)}, bf16[192,768]{1,0:T(8,128)(2,1)S(1)}, u32[]{:S(2)}, u32[]{:S(2)}) collective-permute-start(bf16[192,768]{1,0:T(8,128)(2,1)S(1)} %settle.1.e0_ref), channel_id=1, source_target_pairs={{0,1},{1,0},{2,3},{3,2},{4,5},{5,4},{6,7},{7,6},{8,9},{9,8},{10,11... | collective-permute-start | bytes 884744 | tf_op jit(solution)/shard_map/ppermute | solution.py:31
  98.8 1.6 collective-permute-start.12
  106.8 1.6 copy-start.3
  108.4 1.1 copy-start.4
  109.5 39.7 %copy-start.5 = (bf16[88,1024]{1,0:T(8,128)(2,1)S(1)}, bf16[88,1024]{1,0:T(8,128)(2,1)}, u32[]{:S(2)}) copy-start(bf16[88,1024]{1,0:T(8,128)(2,1)} %p_ref.3) | copy-start | bytes 540676
  109.5 39.7 %all-to-all-start.2 = ((bf16[8,88,2048]{2,1,0:T(8,128)(2,1)}), bf16[8,88,2048]{2,1,0:T(8,128)(2,1)S(1)}, u32[]{:S(2)}, u32[]{:S(2)}) async-start(bf16[8,88,2048]{2,1,0:T(8,128)(2,1)} %bitcast.10), calls=%async_computation.3 | async-start | bytes 5767168 | tf_op jit(solution)/shard_map/all_to_all | solution.py:326
  149.2 0.9 copy-start.7
Sparse Core Ops, SparseCore 0:
  109.6 34.4 reduce-scatter.1

commit v3 on v2

--- a/solution.py
+++ b/solution.py
@@ -60,10 +60,13 @@
     return jnp.concatenate([x, jnp.zeros((PADDED - ROWS, x.shape[1]), x.dtype)])
 
 
-def prepare_kernel(q_ref, p_ref, n_ref, owner_ref, row_ref, q_out_ref, out_ref, turn_ref):
-    for b in range(8):
+def spread_kernel(p_ref, n_ref, out_ref):
+    for b in range(out_ref.shape[0]):
         out_ref[b, :, :FEAT] = p_ref[...]
         out_ref[b, :, FEAT:] = n_ref[...]
+
+
+def pack_kernel(q_ref, owner_ref, row_ref, q_out_ref, turn_ref):
     q_out_ref[:, :FEAT] = pad_rows(q_ref[...].astype(F32)).astype(BF16)
     lane = lax.broadcasted_iota(jnp.int32, (PADDED, 128), 1).astype(F32)
     turn_ref[...] = jnp.zeros((128, 128), F32)
@@ -278,12 +281,21 @@
 
 def local(queries, passages, negatives, neg_owner, neg_row):
     plane = ("y", "xl")
-    packed, spread = blocked(
-        prepare_kernel, "prepare", (queries, passages, negatives, neg_owner.T, neg_row.T),
-        [block((ROWS, FEAT))] * 3 + [block((NEG, ROWS))] * 2,
-        (shaped((PADDED, FEAT + 128), BF16), shaped((8, ROWS, 2 * FEAT), BF16)),
-        scratch=[pltpu.VMEM((128, 128), F32)],
-    )
+    spread = pl.pallas_call(
+        spread_kernel,
+        out_shape=shaped((8, ROWS, 2 * FEAT), BF16),
+        grid=(1,),
+        in_specs=[block((ROWS, FEAT))] * 2,
+        out_specs=pl.BlockSpec((8, ROWS, 2 * FEAT), lambda i: (i, 0, 0)),
+        compiler_params=pltpu.CompilerParams(vmem_limit_bytes=60 * MIB),
+        name="spread",
+    )(passages, negatives)
+    queries, spread = lax.optimization_barrier((queries, spread))
+    packed = blocked(
+        pack_kernel, "prepare", (queries, neg_owner.T, neg_row.T),
+        [block((ROWS, FEAT))] + [block((NEG, ROWS))] * 2,
+        (shaped((PADDED, FEAT + 128), BF16),), scratch=[pltpu.VMEM((128, 128), F32)],
+    )[0]
     pn = lax.all_to_all(spread, plane, 0, 0, tiled=True).reshape(TOTAL, 2 * FEAT)
     pieces = gather_z(packed)
 

time: 161 us -> 160 us (level)
  blocking collectives: 15.7 us -> 12.7 us
    all_to_all x1, blocking collectives: 15.7 us -> 12.7 us  [local(): stats = lax.all_to_all(stats, 'z', 0, 0, tiled=True)]
    pallas_call x0 -> x1, Pallas kernels: none -> 2.74 us  [local(): pl.pallas_call(spread_kernel, out_shape=shaped((8, ROWS, 2 * FEAT), BF16)...]
  transfers between devices with their start and end apart: 16 -> 16, of which waited for: 9 -> 9; matrix products, arithmetic and copies ran while one was open for 0% -> 0% of each run, Pallas kernels for 2% -> 3%
where the time goes in v3:
time: 160 us; the launch traced here: 158 us
  waiting for transfers between devices  74.1 us (46%)
  starting transfers between devices  30.4 us (19%)
  Pallas kernels  18.6 us (12%)
  between operations  14.1 us (9%)
  blocking collectives  12.7 us (8%)
  local copies, waits for them, and re-layouts  7.75 us (5%)
    ppermute x13, waiting for transfers between devices, shift(): lax.ppermute(x, axis, [(i, (i + step) % count) for i in range(count)])  38.6 us
    all_to_all x1, waiting for transfers between devices, local(): lax.all_to_all(gpn.reshape(8, ROWS, 2 * FEAT), plane, 0, 0, tiled=True)  35.4 us
    ppermute x13, starting transfers between devices, shift(): lax.ppermute(x, axis, [(i, (i + step) % count) for i in range(count)])  22.9 us
    all_to_all x1, blocking collectives, local(): stats = lax.all_to_all(stats, 'z', 0, 0, tiled=True)  12.7 us
    pallas_call x6, Pallas kernels, call(): pl.pallas_call(kernel, out_shape=outs, in_specs=[VMEM] * (len(operands) -...  12.6 us
    unnamed x16, local copies, waits for them, and re-layouts  7.22 us
    all_to_all x1, starting transfers between devices, local(): lax.all_to_all(gpn.reshape(8, ROWS, 2 * FEAT), plane, 0, 0, tiled=True)  3.78 us
    all_to_all x1, starting transfers between devices, local(): lax.all_to_all(spread, plane, 0, 0, tiled=True).reshape(TOTAL, 2 * FEAT)  3.66 us
  transfers between devices with their start and end apart: 16, of which 9 were waited for; matrix products, arithmetic and copies ran while one was open for 0% of the time, Pallas kernels for 3%

profile of v3, /device:TPU:0, one launch (start us, length us, event | category | flops | bytes accessed | tf_op | source)
XLA Modules:
  0.0 157.7 jit_solution(4975836436022027817)
XLA Ops:
  7.2 2.7 %spread.1 = bf16[8,88,2048]{2,1,0:T(8,128)(2,1)} custom-call(bf16[88,1024]{1,0:T(8,128)(2,1)} %p_ref.3, bf16[88,1024]{1,0:T(8,128)(2,1)} %n_ref.1), custom_call_target="tpu_custom_call" | custom-call | tf_op jit(solution)/shard_map/spread/pallas_call | solution.py:284
  9.9 3.7 %all-to-all-start = ((bf16[8,88,2048]{2,1,0:T(8,128)(2,1)}), bf16[8,88,2048]{2,1,0:T(8,128)(2,1)S(1)}, u32[]{:S(2)}, u32[]{:S(2)}) async-start(bf16[8,88,2048]{2,1,0:T(8,128)(2,1)} %spread.1), calls=%async_computation | async-start | bytes 5767168 | tf_op jit(solution)/shard_map/all_to_all | solution.py:299
  13.6 0.0 reduce-scatter.2.cloned.1.call-start
  13.6 2.0 %prepare.1.refs_0_ = bf16[96,1152]{1,0:T(8,128)(2,1)} custom-call(bf16[88,1024]{1,0:T(8,128)(2,1)} %q_ref, s32[7,88]{1,0:T(8,128)} %bitcast.12, s32[7,88]{1,0:T(8,128)} %bitcast.13), custom_call_target="tpu_custom_call" | custom-call | tf_op jit(solution)/shard_map/prepare/pallas_call | solution.py:270
  15.6 5.9 %collective-permute-start.4 = (bf16[96,1152]{1,0:T(8,128)(2,1)}, bf16[96,1152]{1,0:T(8,128)(2,1)S(1)}, u32[]{:S(2)}, u32[]{:S(2)}) collective-permute-start(bf16[96,1152]{1,0:T(8,128)(2,1)} %prepare.1.refs_0_), channel_id=1, source_target_pairs={{0,56},{8,0},{16,8},{24,16},{32,24},{40,32},{48,40},{56,48},{1,57}... | collective-permute-start | bytes 663560 | tf_op jit(solution)/shard_map/ppermute | solution.py:31
  21.4 0.0 collective-permute-start
  21.4 4.7 %collective-permute-done.4.refs_8_ = bf16[96,1152]{1,0:T(8,128)(2,1)S(1)} collective-permute-done((bf16[96,1152]{1,0:T(8,128)(2,1)}, bf16[96,1152]{1,0:T(8,128)(2,1)S(1)}, u32[]{:S(2)}, u32[]{:S(2)}) %collective-permute-start.4) | collective-permute-done | bytes 221216 | tf_op jit(solution)/shard_map/ppermute | solution.py:31
  26.2 3.6 %collective-permute-start.5 = (bf16[96,1152]{1,0:T(8,128)(2,1)S(1)}, bf16[96,1152]{1,0:T(8,128)(2,1)S(1)}, u32[]{:S(2)}, u32[]{:S(2)}) collective-permute-start(bf16[96,1152]{1,0:T(8,128)(2,1)S(1)} %collective-permute-done.4.refs_8_), channel_id=1, source_target_pairs={{0,56},{8,0},{16,8},{24,16},{32,24},{40,32},{48,40},{56,48},{1,57}... | collective-permute-start | bytes 663560 | tf_op jit(solution)/shard_map/ppermute | solution.py:31
  29.8 0.0 collective-permute-done.refs_1_
  29.8 0.0 collective-permute-start.1
  29.8 3.5 %collective-permute-done.5.refs_7_ = bf16[96,1152]{1,0:T(8,128)(2,1)S(1)} collective-permute-done((bf16[96,1152]{1,0:T(8,128)(2,1)S(1)}, bf16[96,1152]{1,0:T(8,128)(2,1)S(1)}, u32[]{:S(2)}, u32[]{:S(2)}) %collective-permute-start.5) | collective-permute-done | bytes 221216 | tf_op jit(solution)/shard_map/ppermute | solution.py:31
  33.3 3.7 %collective-permute-start.6 = (bf16[96,1152]{1,0:T(8,128)(2,1)S(1)}, bf16[96,1152]{1,0:T(8,128)(2,1)S(1)}, u32[]{:S(2)}, u32[]{:S(2)}) collective-permute-start(bf16[96,1152]{1,0:T(8,128)(2,1)S(1)} %collective-permute-done.5.refs_7_), channel_id=1, source_target_pairs={{0,56},{8,0},{16,8},{24,16},{32,24},{40,32},{48,40},{56,48},{1,57}... | collective-permute-start | bytes 663560 | tf_op jit(solution)/shard_map/ppermute | solution.py:31
  36.9 0.0 collective-permute-done.1.refs_2_
  36.9 0.0 collective-permute-start.2
  37.0 3.4 %collective-permute-done.6.refs_6_ = bf16[96,1152]{1,0:T(8,128)(2,1)S(1)} collective-permute-done((bf16[96,1152]{1,0:T(8,128)(2,1)S(1)}, bf16[96,1152]{1,0:T(8,128)(2,1)S(1)}, u32[]{:S(2)}, u32[]{:S(2)}) %collective-permute-start.6) | collective-permute-done | bytes 221216 | tf_op jit(solution)/shard_map/ppermute | solution.py:31
  40.4 3.8 %collective-permute-start.7 = (bf16[48,1152]{1,0:T(8,128)(2,1)S(1)}, bf16[48,1152]{1,0:T(8,128)(2,1)S(1)}, u32[]{:S(2)}, u32[]{:S(2)}) collective-permute-start(bf16[48,1152]{1,0:T(8,128)(2,1)S(1)} %slice.21), channel_id=1, source_target_pairs={{0,56},{8,0},{16,8},{24,16},{32,24},{40,32},{48,40},{56,48},{1,57}... | collective-permute-start | bytes 331784 | tf_op jit(solution)/shard_map/ppermute | solution.py:31
  44.2 0.0 collective-permute-done.2.refs_3_
  44.2 0.1 collective-permute-start.3
  44.3 2.2 %collective-permute-done.7.refs_5_ = bf16[48,1152]{1,0:T(8,128)(2,1)S(1)} collective-permute-done((bf16[48,1152]{1,0:T(8,128)(2,1)S(1)}, bf16[48,1152]{1,0:T(8,128)(2,1)S(1)}, u32[]{:S(2)}, u32[]{:S(2)}) %collective-permute-start.7) | collective-permute-done | bytes 110624 | tf_op jit(solution)/shard_map/ppermute | solution.py:31
  46.5 3.7 %collective-permute-done.3.refs_4_ = bf16[48,1152]{1,0:T(8,128)(2,1)S(1)} collective-permute-done((bf16[48,1152]{1,0:T(8,128)(2,1)S(1)}, bf16[48,1152]{1,0:T(8,128)(2,1)S(1)}, u32[]{:S(2)}, u32[]{:S(2)}) %collective-permute-start.3) | collective-permute-done | bytes 110624 | tf_op jit(solution)/shard_map/ppermute | solution.py:31
  50.2 0.0 copy-start.5
  50.2 0.9 copy-done.5
  51.2 0.1 join.1.q_ref
  51.3 0.0 copy-start
  51.3 1.2 copy-done
  52.6 0.0 all-to-all-done
  52.6 0.0 copy-start.1
  52.6 1.5 copy-done.1
  54.0 2.7 %scores_give.1 = f32[2,176,768]{2,1,0:T(8,128)S(1)} custom-call(bf16[768,1152]{1,0:T(8,128)(2,1)S(1)} %copy-done.1, bf16[704,2048]{1,0:T(8,128)(2,1)S(1)} %bitcast.7), custom_call_target="tpu_custom_call" | custom-call | bytes 1024 | tf_op jit(solution)/shard_map/scores_give/pallas_call | solution.py:257
  56.7 0.3 collective-permute-start.8
  57.0 2.7 %scores_keep.1.keep_ref = f32[2,176,768]{2,1,0:T(8,128)S(1)} custom-call(bf16[768,1152]{1,0:T(8,128)(2,1)S(1)} %copy-done.1, bf16[704,2048]{1,0:T(8,128)(2,1)S(1)} %bitcast.8), custom_call_target="tpu_custom_call" | custom-call | bytes 1024 | tf_op jit(solution)/shard_map/scores_keep/pallas_call | solution.py:257
  59.7 0.0 collective-permute-done.8.near_ref
  59.7 0.1 slice_add_fusion
  59.8 0.0 copy-start.2
  59.8 2.8 %collective-permute-start.9 = (f32[1,176,768]{2,1,0:T(8,128)S(1)}, f32[1,176,768]{2,1,0:T(8,128)S(1)}, u32[]{:S(2)}, u32[]{:S(2)}) collective-permute-start(f32[1,176,768]{2,1,0:T(8,128)S(1)} %slice_add_fusion), channel_id=1, source_target_pairs={{0,2},{2,0},{1,3},{3,1},{4,6},{6,4},{5,7},{7,5},{8,10},{10,8},{9,1... | collective-permute-start | bytes 1622024 | tf_op jit(solution)/shard_map/ppermute | solution.py:31
  62.6 13.4 %collective-permute-done.9.far_ref = f32[1,176,768]{2,1,0:T(8,128)S(1)} collective-permute-done((f32[1,176,768]{2,1,0:T(8,128)S(1)}, f32[1,176,768]{2,1,0:T(8,128)S(1)}, u32[]{:S(2)}, u32[]{:S(2)}) %collective-permute-start.9) | collective-permute-done | bytes 540704 | tf_op jit(solution)/shard_map/ppermute | solution.py:31
  76.0 0.4 soft.1
  76.4 12.7 %all_to_all.15.stats_ref = f32[8,8,128]{2,1,0:T(8,128)S(1)} all-to-all(f32[8,8,128]{2,1,0:T(8,128)S(1)} %get-tuple-element.17), channel_id=1, replica_groups=mesh['y'=4,'z'=8,'xl'=2,'xh'=2,'c'=2] {'z'}, dimensions={0} | all-to-all | bytes 65536 | tf_op jit(solution)/shard_map/all_to_all | solution.py:319
  89.1 0.3 settle.1.e0_ref
  89.4 2.8 %collective-permute-start.11 = (bf16[192,768]{1,0:T(8,128)(2,1)S(1)}, bf16[192,768]{1,0:T(8,128)(2,1)S(1)}, u32[]{:S(2)}, u32[]{:S(2)}) collective-permute-start(bf16[192,768]{1,0:T(8,128)(2,1)S(1)} %settle.1.e0_ref), channel_id=1, source_target_pairs={{0,2},{2,0},{1,3},{3,1},{4,6},{6,4},{5,7},{7,5},{8,10},{10,8},{9,1... | collective-permute-start | bytes 884744 | tf_op jit(solution)/shard_map/ppermute | solution.py:31
  92.3 0.0 collective-permute-start.10
  92.3 6.0 %collective-permute-done.11.e2_ref = bf16[192,768]{1,0:T(8,128)(2,1)S(1)} collective-permute-done((bf16[192,768]{1,0:T(8,128)(2,1)S(1)}, bf16[192,768]{1,0:T(8,128)(2,1)S(1)}, u32[]{:S(2)}, u32[]{:S(2)}) %collective-permute-start.11) | collective-permute-done | bytes 294944 | tf_op jit(solution)/shard_map/ppermute | solution.py:31
  98.2 0.0 collective-permute-start.12
  98.2 0.0 collective-permute-done.10.e1_ref
  98.2 1.6 collective-permute-done.12.e3_ref
  99.8 0.0 copy-done.2
  99.8 6.4 %weights.1 = (bf16[704,2048]{1,0:T(8,128)(2,1)S(1)}, bf16[8,88,1024]{2,1,0:T(8,128)(2,1)S(1)}, f32[8,128]{1,0:T(8,128)S(1)}, f32[96,128]{1,0:T(8,128)S(1)}) custom-call(bf16[192,768]{1,0:T(8,128)(2,1)S(1)} %settle.1.e0_ref, bf16[192,768]{1,0:T(8,128)(2,1)S(1)} %collective-permute-done.10.e1_ref, bf16[192,768]{1,0:T(8,128)(2,1)S(1)} %collective-permute-done.11.e2_ref, ...), custom_call_target="tpu_custom_call" | custom-call | bytes 1024 | tf_op jit(solution)/shard_map/weights/pallas_call | solution.py:257
  106.2 0.0 copy-start.3
  106.2 1.5 copy-done.3
  107.8 0.0 copy-start.4
  107.8 1.1 copy-done.4
  108.9 0.0 reduce-scatter.2.cloned.1.call-update
  108.9 0.0 copy-start.6
  108.9 3.8 %all-to-all-start.2 = ((bf16[8,88,2048]{2,1,0:T(8,128)(2,1)}), bf16[8,88,2048]{2,1,0:T(8,128)(2,1)S(1)}, u32[]{:S(2)}, u32[]{:S(2)}) async-start(bf16[8,88,2048]{2,1,0:T(8,128)(2,1)} %bitcast.10), calls=%async_computation.3 | async-start | bytes 5767168 | tf_op jit(solution)/shard_map/all_to_all | solution.py:338
  112.7 0.5 slice_bitcast_fusion
  113.2 35.4 %all-to-all-done.2.x_ref = bf16[8,88,2048]{2,1,0:T(8,128)(2,1)S(1)} async-done(((bf16[8,88,2048]{2,1,0:T(8,128)(2,1)}), bf16[8,88,2048]{2,1,0:T(8,128)(2,1)S(1)}, u32[]{:S(2)}, u32[]{:S(2)}) %all-to-all-start.2) | async-done | bytes 2883616 | tf_op jit(solution)/shard_map/all_to_all | solution.py:338
  148.6 0.0 reduce-scatter.2.cloned.1.call-done
  148.6 0.0 copy-done.6
  148.7 0.0 copy-start.7
  148.7 0.9 copy-done.7
  149.6 1.3 finish.1
  (2 shorter events, 0.0 us)
Async XLA Ops:
  9.9 42.7 %all-to-all-start = ((bf16[8,88,2048]{2,1,0:T(8,128)(2,1)}), bf16[8,88,2048]{2,1,0:T(8,128)(2,1)S(1)}, u32[]{:S(2)}, u32[]{:S(2)}) async-start(bf16[8,88,2048]{2,1,0:T(8,128)(2,1)} %spread.1), calls=%async_computation | async-start | bytes 5767168 | tf_op jit(solution)/shard_map/all_to_all | solution.py:299
  13.6 135.1 %reduce-scatter.2.cloned.1.call-start = ((), (), s32[]{:S(2)}) async-start(), calls=%async_computation.4 | async-start | bytes 1622016 | tf_op jit(solution)/shard_map/reduce_scatter | solution.py:337
  15.6 10.6 %collective-permute-start.4 = (bf16[96,1152]{1,0:T(8,128)(2,1)}, bf16[96,1152]{1,0:T(8,128)(2,1)S(1)}, u32[]{:S(2)}, u32[]{:S(2)}) collective-permute-start(bf16[96,1152]{1,0:T(8,128)(2,1)} %prepare.1.refs_0_), channel_id=1, source_target_pairs={{0,56},{8,0},{16,8},{24,16},{32,24},{40,32},{48,40},{56,48},{1,57}... | collective-permute-start | bytes 663560 | tf_op jit(solution)/shard_map/ppermute | solution.py:31
  21.4 8.3 %collective-permute-start = (bf16[96,1152]{1,0:T(8,128)(2,1)}, bf16[96,1152]{1,0:T(8,128)(2,1)S(1)}, u32[]{:S(2)}, u32[]{:S(2)}) collective-permute-start(bf16[96,1152]{1,0:T(8,128)(2,1)} %prepare.1.refs_0_), channel_id=1, source_target_pairs={{0,8},{8,16},{16,24},{24,32},{32,40},{40,48},{48,56},{56,0},{1,9},... | collective-permute-start | bytes 663560 | tf_op jit(solution)/shard_map/ppermute | solution.py:31
  26.2 7.1 %collective-permute-start.5 = (bf16[96,1152]{1,0:T(8,128)(2,1)S(1)}, bf16[96,1152]{1,0:T(8,128)(2,1)S(1)}, u32[]{:S(2)}, u32[]{:S(2)}) collective-permute-start(bf16[96,1152]{1,0:T(8,128)(2,1)S(1)} %collective-permute-done.4.refs_8_), channel_id=1, source_target_pairs={{0,56},{8,0},{16,8},{24,16},{32,24},{40,32},{48,40},{56,48},{1,57}... | collective-permute-start | bytes 663560 | tf_op jit(solution)/shard_map/ppermute | solution.py:31
  29.8 7.2 %collective-permute-start.1 = (bf16[96,1152]{1,0:T(8,128)(2,1)S(1)}, bf16[96,1152]{1,0:T(8,128)(2,1)S(1)}, u32[]{:S(2)}, u32[]{:S(2)}) collective-permute-start(bf16[96,1152]{1,0:T(8,128)(2,1)S(1)} %collective-permute-done.refs_1_), channel_id=1, source_target_pairs={{0,8},{8,16},{16,24},{24,32},{32,40},{40,48},{48,56},{56,0},{1,9},... | collective-permute-start | bytes 663560 | tf_op jit(solution)/shard_map/ppermute | solution.py:31
  33.3 7.1 %collective-permute-start.6 = (bf16[96,1152]{1,0:T(8,128)(2,1)S(1)}, bf16[96,1152]{1,0:T(8,128)(2,1)S(1)}, u32[]{:S(2)}, u32[]{:S(2)}) collective-permute-start(bf16[96,1152]{1,0:T(8,128)(2,1)S(1)} %collective-permute-done.5.refs_7_), channel_id=1, source_target_pairs={{0,56},{8,0},{16,8},{24,16},{32,24},{40,32},{48,40},{56,48},{1,57}... | collective-permute-start | bytes 663560 | tf_op jit(solution)/shard_map/ppermute | solution.py:31
  36.9 7.2 %collective-permute-start.2 = (bf16[96,1152]{1,0:T(8,128)(2,1)S(1)}, bf16[96,1152]{1,0:T(8,128)(2,1)S(1)}, u32[]{:S(2)}, u32[]{:S(2)}) collective-permute-start(bf16[96,1152]{1,0:T(8,128)(2,1)S(1)} %collective-permute-done.1.refs_2_), channel_id=1, source_target_pairs={{0,8},{8,16},{16,24},{24,32},{32,40},{40,48},{48,56},{56,0},{1,9},... | collective-permute-start | bytes 663560 | tf_op jit(solution)/shard_map/ppermute | solution.py:31
  40.4 6.1 %collective-permute-start.7 = (bf16[48,1152]{1,0:T(8,128)(2,1)S(1)}, bf16[48,1152]{1,0:T(8,128)(2,1)S(1)}, u32[]{:S(2)}, u32[]{:S(2)}) collective-permute-start(bf16[48,1152]{1,0:T(8,128)(2,1)S(1)} %slice.21), channel_id=1, source_target_pairs={{0,56},{8,0},{16,8},{24,16},{32,24},{40,32},{48,40},{56,48},{1,57}... | collective-permute-start | bytes 331784 | tf_op jit(solution)/shard_map/ppermute | solution.py:31
  44.2 6.0 %collective-permute-start.3 = (bf16[48,1152]{1,0:T(8,128)(2,1)S(1)}, bf16[48,1152]{1,0:T(8,128)(2,1)S(1)}, u32[]{:S(2)}, u32[]{:S(2)}) collective-permute-start(bf16[48,1152]{1,0:T(8,128)(2,1)S(1)} %slice.20), channel_id=1, source_target_pairs={{0,8},{8,16},{16,24},{24,32},{32,40},{40,48},{48,56},{56,0},{1,9},... | collective-permute-start | bytes 331784 | tf_op jit(solution)/shard_map/ppermute | solution.py:31
  50.2 0.9 copy-start.5
  51.3 1.2 copy-start
  52.6 1.5 copy-start.1
  56.7 3.0 %collective-permute-start.8 = (f32[2,176,768]{2,1,0:T(8,128)S(1)}, f32[2,176,768]{2,1,0:T(8,128)S(1)}, u32[]{:S(2)}, u32[]{:S(2)}) collective-permute-start(f32[2,176,768]{2,1,0:T(8,128)S(1)} %scores_give.1), channel_id=1, source_target_pairs={{0,1},{1,0},{2,3},{3,2},{4,5},{5,4},{6,7},{7,6},{8,9},{9,8},{10,11... | collective-permute-start | bytes 3244040 | tf_op jit(solution)/shard_map/ppermute | solution.py:31
  59.8 40.1 %copy-start.2 = (bf16[768,1152]{1,0:T(8,128)(2,1)S(1)}, bf16[768,1152]{1,0:T(8,128)(2,1)}, u32[]{:S(2)}) copy-start(bf16[768,1152]{1,0:T(8,128)(2,1)} %copy-done) | copy-start | bytes 5308420
  59.8 16.3 %collective-permute-start.9 = (f32[1,176,768]{2,1,0:T(8,128)S(1)}, f32[1,176,768]{2,1,0:T(8,128)S(1)}, u32[]{:S(2)}, u32[]{:S(2)}) collective-permute-start(f32[1,176,768]{2,1,0:T(8,128)S(1)} %slice_add_fusion), channel_id=1, source_target_pairs={{0,2},{2,0},{1,3},{3,1},{4,6},{6,4},{5,7},{7,5},{8,10},{10,8},{9,1... | collective-permute-start | bytes 1622024 | tf_op jit(solution)/shard_map/ppermute | solution.py:31
  89.4 8.8 %collective-permute-start.11 = (bf16[192,768]{1,0:T(8,128)(2,1)S(1)}, bf16[192,768]{1,0:T(8,128)(2,1)S(1)}, u32[]{:S(2)}, u32[]{:S(2)}) collective-permute-start(bf16[192,768]{1,0:T(8,128)(2,1)S(1)} %settle.1.e0_ref), channel_id=1, source_target_pairs={{0,2},{2,0},{1,3},{3,1},{4,6},{6,4},{5,7},{7,5},{8,10},{10,8},{9,1... | collective-permute-start | bytes 884744 | tf_op jit(solution)/shard_map/ppermute | solution.py:31
  92.3 6.0 %collective-permute-start.10 = (bf16[192,768]{1,0:T(8,128)(2,1)S(1)}, bf16[192,768]{1,0:T(8,128)(2,1)S(1)}, u32[]{:S(2)}, u32[]{:S(2)}) collective-permute-start(bf16[192,768]{1,0:T(8,128)(2,1)S(1)} %settle.1.e0_ref), channel_id=1, source_target_pairs={{0,1},{1,0},{2,3},{3,2},{4,5},{5,4},{6,7},{7,6},{8,9},{9,8},{10,11... | collective-permute-start | bytes 884744 | tf_op jit(solution)/shard_map/ppermute | solution.py:31
  98.2 1.6 %collective-permute-start.12 = (bf16[192,768]{1,0:T(8,128)(2,1)S(1)}, bf16[192,768]{1,0:T(8,128)(2,1)S(1)}, u32[]{:S(2)}, u32[]{:S(2)}) collective-permute-start(bf16[192,768]{1,0:T(8,128)(2,1)S(1)} %collective-permute-done.11.e2_ref), channel_id=1, source_target_pairs={{0,1},{1,0},{2,3},{3,2},{4,5},{5,4},{6,7},{7,6},{8,9},{9,8},{10,11... | collective-permute-start | bytes 884744 | tf_op jit(solution)/shard_map/ppermute | solution.py:31
  106.2 1.5 copy-start.3
  107.8 1.1 copy-start.4
  108.9 39.7 %copy-start.6 = (bf16[88,1024]{1,0:T(8,128)(2,1)S(1)}, bf16[88,1024]{1,0:T(8,128)(2,1)}, u32[]{:S(2)}) copy-start(bf16[88,1024]{1,0:T(8,128)(2,1)} %p_ref.3) | copy-start | bytes 540676
  108.9 39.7 %all-to-all-start.2 = ((bf16[8,88,2048]{2,1,0:T(8,128)(2,1)}), bf16[8,88,2048]{2,1,0:T(8,128)(2,1)S(1)}, u32[]{:S(2)}, u32[]{:S(2)}) async-start(bf16[8,88,2048]{2,1,0:T(8,128)(2,1)} %bitcast.10), calls=%async_computation.3 | async-start | bytes 5767168 | tf_op jit(solution)/shard_map/all_to_all | solution.py:338
  148.7 0.9 copy-start.7
Sparse Core Ops, SparseCore 0:
  109.0 34.4 reduce-scatter.1

commit v4 on v2

--- a/solution.py
+++ b/solution.py
@@ -310,6 +310,7 @@
         [pltpu.VMEM((128, 128), F32)],
     )[0]
     e2 = shift(e0, "xh", 2, 1)
+    e0, e2 = lax.optimization_barrier((e0, e2))
     e1 = shift(e0, "c", 2, 1)
     e3 = shift(e2, "c", 2, 1)
 

time: 161 us -> 161 us (level)
  transfers between devices with their start and end apart: 16 -> 16, of which waited for: 9 -> 10; matrix products, arithmetic and copies ran while one was open for 0% -> 0% of each run, Pallas kernels for 2% -> 2%
where the time goes in v4:
time: 161 us; the launch traced here: 159 us
  waiting for transfers between devices  73.6 us (46%)
  starting transfers between devices  31.2 us (19%)
  Pallas kernels  17.1 us (11%)
  blocking collectives  15.7 us (10%)
  between operations  14.2 us (9%)
  local copies, waits for them, and re-layouts  6.86 us (4%)
    ppermute x13, waiting for transfers between devices, shift(): lax.ppermute(x, axis, [(i, (i + step) % count) for i in range(count)])  38.2 us
    all_to_all x1, waiting for transfers between devices, local(): lax.all_to_all(gpn.reshape(8, ROWS, 2 * FEAT), plane, 0, 0, tiled=True)  35.4 us
    ppermute x13, starting transfers between devices, shift(): lax.ppermute(x, axis, [(i, (i + step) % count) for i in range(count)])  23.6 us
    all_to_all x1, blocking collectives, local(): stats = lax.all_to_all(stats, 'z', 0, 0, tiled=True)  15.7 us
    pallas_call x6, Pallas kernels, call(): pl.pallas_call(kernel, out_shape=outs, in_specs=[VMEM] * (len(operands) -...  12.6 us
    unnamed x16, local copies, waits for them, and re-layouts  6.33 us
    pallas_call x2, Pallas kernels, blocked(): pl.pallas_call(kernel, out_shape=outs, grid=(1,), in_specs=in_specs, out_...  4.49 us
    all_to_all x1, starting transfers between devices, local(): lax.all_to_all(spread, plane, 0, 0, tiled=True).reshape(TOTAL, 2 * FEAT)  3.79 us
  transfers between devices with their start and end apart: 16, of which 10 were waited for; matrix products, arithmetic and copies ran while one was open for 0% of the time, Pallas kernels for 2%

profile of v4, /device:TPU:0, one launch (start us, length us, event | category | flops | bytes accessed | tf_op | source)
XLA Modules:
  0.0 158.7 jit_solution(1759779911839983471)
XLA Ops:
  7.2 3.2 %prepare.1 = (bf16[96,1152]{1,0:T(8,128)(2,1)}, bf16[8,88,2048]{2,1,0:T(8,128)(2,1)}) custom-call(bf16[88,1024]{1,0:T(8,128)(2,1)} %q_ref.1, bf16[88,1024]{1,0:T(8,128)(2,1)} %p_ref.3, bf16[88,1024]{1,0:T(8,128)(2,1)} %n_ref.1, s32[7,88]{1,0:T(8,128)} %bitcast.12, s32[7,88]{1,0:T(8,128)} %bitcast.13), custom_call_target="tpu_custom_call" | custom-call | tf_op jit(solution)/shard_map/prepare/pallas_call | solution.py:267
  10.4 0.0 copy-start.6
  10.4 3.8 %all-to-all-start = ((bf16[8,88,2048]{2,1,0:T(8,128)(2,1)}), bf16[8,88,2048]{2,1,0:T(8,128)(2,1)S(1)}, u32[]{:S(2)}, u32[]{:S(2)}) async-start(bf16[8,88,2048]{2,1,0:T(8,128)(2,1)} %get-tuple-element.18), calls=%async_computation | async-start | bytes 5767168 | tf_op jit(solution)/shard_map/all_to_all | solution.py:287
  14.1 0.0 reduce-scatter.2.cloned.1.call-start
  14.2 0.0 copy-done.6
  14.2 5.9 %collective-permute-start.4 = (bf16[96,1152]{1,0:T(8,128)(2,1)S(1)}, bf16[96,1152]{1,0:T(8,128)(2,1)S(1)}, u32[]{:S(2)}, u32[]{:S(2)}) collective-permute-start(bf16[96,1152]{1,0:T(8,128)(2,1)S(1)} %copy-done.6), channel_id=1, source_target_pairs={{0,56},{8,0},{16,8},{24,16},{32,24},{40,32},{48,40},{56,48},{1,57}... | collective-permute-start | bytes 663560 | tf_op jit(solution)/shard_map/ppermute | solution.py:31
  20.1 0.0 collective-permute-start
  20.1 4.4 %collective-permute-done.4.refs_8_ = bf16[96,1152]{1,0:T(8,128)(2,1)S(1)} collective-permute-done((bf16[96,1152]{1,0:T(8,128)(2,1)S(1)}, bf16[96,1152]{1,0:T(8,128)(2,1)S(1)}, u32[]{:S(2)}, u32[]{:S(2)}) %collective-permute-start.4) | collective-permute-done | bytes 221216 | tf_op jit(solution)/shard_map/ppermute | solution.py:31
  24.5 3.7 %collective-permute-start.5 = (bf16[96,1152]{1,0:T(8,128)(2,1)S(1)}, bf16[96,1152]{1,0:T(8,128)(2,1)S(1)}, u32[]{:S(2)}, u32[]{:S(2)}) collective-permute-start(bf16[96,1152]{1,0:T(8,128)(2,1)S(1)} %collective-permute-done.4.refs_8_), channel_id=1, source_target_pairs={{0,56},{8,0},{16,8},{24,16},{32,24},{40,32},{48,40},{56,48},{1,57}... | collective-permute-start | bytes 663560 | tf_op jit(solution)/shard_map/ppermute | solution.py:31
  28.2 0.0 collective-permute-done.refs_1_
  28.2 0.0 collective-permute-start.1
  28.2 3.5 %collective-permute-done.5.refs_7_ = bf16[96,1152]{1,0:T(8,128)(2,1)S(1)} collective-permute-done((bf16[96,1152]{1,0:T(8,128)(2,1)S(1)}, bf16[96,1152]{1,0:T(8,128)(2,1)S(1)}, u32[]{:S(2)}, u32[]{:S(2)}) %collective-permute-start.5) | collective-permute-done | bytes 221216 | tf_op jit(solution)/shard_map/ppermute | solution.py:31
  31.7 3.7 %collective-permute-start.6 = (bf16[96,1152]{1,0:T(8,128)(2,1)S(1)}, bf16[96,1152]{1,0:T(8,128)(2,1)S(1)}, u32[]{:S(2)}, u32[]{:S(2)}) collective-permute-start(bf16[96,1152]{1,0:T(8,128)(2,1)S(1)} %collective-permute-done.5.refs_7_), channel_id=1, source_target_pairs={{0,56},{8,0},{16,8},{24,16},{32,24},{40,32},{48,40},{56,48},{1,57}... | collective-permute-start | bytes 663560 | tf_op jit(solution)/shard_map/ppermute | solution.py:31
  35.4 0.0 collective-permute-done.1.refs_2_
  35.4 0.0 collective-permute-start.2
  35.4 3.4 %collective-permute-done.6.refs_6_ = bf16[96,1152]{1,0:T(8,128)(2,1)S(1)} collective-permute-done((bf16[96,1152]{1,0:T(8,128)(2,1)S(1)}, bf16[96,1152]{1,0:T(8,128)(2,1)S(1)}, u32[]{:S(2)}, u32[]{:S(2)}) %collective-permute-start.6) | collective-permute-done | bytes 221216 | tf_op jit(solution)/shard_map/ppermute | solution.py:31
  38.9 3.8 %collective-permute-start.7 = (bf16[48,1152]{1,0:T(8,128)(2,1)S(1)}, bf16[48,1152]{1,0:T(8,128)(2,1)S(1)}, u32[]{:S(2)}, u32[]{:S(2)}) collective-permute-start(bf16[48,1152]{1,0:T(8,128)(2,1)S(1)} %slice.21), channel_id=1, source_target_pairs={{0,56},{8,0},{16,8},{24,16},{32,24},{40,32},{48,40},{56,48},{1,57}... | collective-permute-start | bytes 331784 | tf_op jit(solution)/shard_map/ppermute | solution.py:31
  42.7 0.0 collective-permute-done.2.refs_3_
  42.7 0.1 collective-permute-start.3
  42.8 2.2 %collective-permute-done.7.refs_5_ = bf16[48,1152]{1,0:T(8,128)(2,1)S(1)} collective-permute-done((bf16[48,1152]{1,0:T(8,128)(2,1)S(1)}, bf16[48,1152]{1,0:T(8,128)(2,1)S(1)}, u32[]{:S(2)}, u32[]{:S(2)}) %collective-permute-start.7) | collective-permute-done | bytes 110624 | tf_op jit(solution)/shard_map/ppermute | solution.py:31
  45.0 3.7 %collective-permute-done.3.refs_4_ = bf16[48,1152]{1,0:T(8,128)(2,1)S(1)} collective-permute-done((bf16[48,1152]{1,0:T(8,128)(2,1)S(1)}, bf16[48,1152]{1,0:T(8,128)(2,1)S(1)}, u32[]{:S(2)}, u32[]{:S(2)}) %collective-permute-start.3) | collective-permute-done | bytes 110624 | tf_op jit(solution)/shard_map/ppermute | solution.py:31
  48.7 0.1 join.1.q_ref
  48.9 0.0 copy-start
  48.9 1.2 copy-done
  50.1 0.0 all-to-all-done
  50.1 0.0 copy-start.1
  50.1 1.5 copy-done.1
  51.6 2.7 %scores_give.1 = f32[2,176,768]{2,1,0:T(8,128)S(1)} custom-call(bf16[768,1152]{1,0:T(8,128)(2,1)S(1)} %copy-done.1, bf16[704,2048]{1,0:T(8,128)(2,1)S(1)} %bitcast.7), custom_call_target="tpu_custom_call" | custom-call | bytes 1024 | tf_op jit(solution)/shard_map/scores_give/pallas_call | solution.py:254
  54.3 0.3 collective-permute-start.8
  54.6 2.7 %scores_keep.1.keep_ref = f32[2,176,768]{2,1,0:T(8,128)S(1)} custom-call(bf16[768,1152]{1,0:T(8,128)(2,1)S(1)} %copy-done.1, bf16[704,2048]{1,0:T(8,128)(2,1)S(1)} %bitcast.8), custom_call_target="tpu_custom_call" | custom-call | bytes 1024 | tf_op jit(solution)/shard_map/scores_keep/pallas_call | solution.py:254
  57.2 0.0 collective-permute-done.8.near_ref
  57.3 0.1 slice_add_fusion
  57.3 0.0 copy-start.2
  57.3 2.8 %collective-permute-start.9 = (f32[1,176,768]{2,1,0:T(8,128)S(1)}, f32[1,176,768]{2,1,0:T(8,128)S(1)}, u32[]{:S(2)}, u32[]{:S(2)}) collective-permute-start(f32[1,176,768]{2,1,0:T(8,128)S(1)} %slice_add_fusion), channel_id=1, source_target_pairs={{0,2},{2,0},{1,3},{3,1},{4,6},{6,4},{5,7},{7,5},{8,10},{10,8},{9,1... | collective-permute-start | bytes 1622024 | tf_op jit(solution)/shard_map/ppermute | solution.py:31
  60.1 13.5 %collective-permute-done.9.far_ref = f32[1,176,768]{2,1,0:T(8,128)S(1)} collective-permute-done((f32[1,176,768]{2,1,0:T(8,128)S(1)}, f32[1,176,768]{2,1,0:T(8,128)S(1)}, u32[]{:S(2)}, u32[]{:S(2)}) %collective-permute-start.9) | collective-permute-done | bytes 540704 | tf_op jit(solution)/shard_map/ppermute | solution.py:31
  73.6 0.4 soft.1
  74.0 15.7 %all_to_all.15.stats_ref = f32[8,8,128]{2,1,0:T(8,128)S(1)} all-to-all(f32[8,8,128]{2,1,0:T(8,128)S(1)} %get-tuple-element.19), channel_id=1, replica_groups=mesh['y'=4,'z'=8,'xl'=2,'xh'=2,'c'=2] {'z'}, dimensions={0} | all-to-all | bytes 65536 | tf_op jit(solution)/shard_map/all_to_all | solution.py:307
  89.7 0.3 settle.1.e0_ref
  90.0 2.8 %collective-permute-start.10 = (bf16[192,768]{1,0:T(8,128)(2,1)S(1)}, bf16[192,768]{1,0:T(8,128)(2,1)S(1)}, u32[]{:S(2)}, u32[]{:S(2)}) collective-permute-start(bf16[192,768]{1,0:T(8,128)(2,1)S(1)} %settle.1.e0_ref), channel_id=1, source_target_pairs={{0,2},{2,0},{1,3},{3,1},{4,6},{6,4},{5,7},{7,5},{8,10},{10,8},{9,1... | collective-permute-start | bytes 884744 | tf_op jit(solution)/shard_map/ppermute | solution.py:31
  92.8 6.0 %collective-permute-done.10.e2_ref = bf16[192,768]{1,0:T(8,128)(2,1)S(1)} collective-permute-done((bf16[192,768]{1,0:T(8,128)(2,1)S(1)}, bf16[192,768]{1,0:T(8,128)(2,1)S(1)}, u32[]{:S(2)}, u32[]{:S(2)}) %collective-permute-start.10) | collective-permute-done | bytes 294944 | tf_op jit(solution)/shard_map/ppermute | solution.py:31
  98.8 0.0 collective-permute-start.11
  98.8 0.5 collective-permute-start.12
  99.3 1.1 collective-permute-done.11.e1_ref
  100.4 0.4 collective-permute-done.12.e3_ref
  100.8 0.0 copy-done.2
  100.8 6.4 %weights.1 = (bf16[704,2048]{1,0:T(8,128)(2,1)S(1)}, bf16[8,88,1024]{2,1,0:T(8,128)(2,1)S(1)}, f32[8,128]{1,0:T(8,128)S(1)}, f32[96,128]{1,0:T(8,128)S(1)}) custom-call(bf16[192,768]{1,0:T(8,128)(2,1)S(1)} %settle.1.e0_ref, bf16[192,768]{1,0:T(8,128)(2,1)S(1)} %collective-permute-done.11.e1_ref, bf16[192,768]{1,0:T(8,128)(2,1)S(1)} %collective-permute-done.10.e2_ref, ...), custom_call_target="tpu_custom_call" | custom-call | bytes 1024 | tf_op jit(solution)/shard_map/weights/pallas_call | solution.py:254
  107.2 0.0 copy-start.3
  107.2 1.5 copy-done.3
  108.8 0.0 copy-start.4
  108.8 1.1 copy-done.4
  109.9 0.0 reduce-scatter.2.cloned.1.call-update
  109.9 0.0 copy-start.5
  110.0 3.8 %all-to-all-start.2 = ((bf16[8,88,2048]{2,1,0:T(8,128)(2,1)}), bf16[8,88,2048]{2,1,0:T(8,128)(2,1)S(1)}, u32[]{:S(2)}, u32[]{:S(2)}) async-start(bf16[8,88,2048]{2,1,0:T(8,128)(2,1)} %bitcast.10), calls=%async_computation.3 | async-start | bytes 5767168 | tf_op jit(solution)/shard_map/all_to_all | solution.py:327
  113.7 0.5 slice_bitcast_fusion
  114.3 35.4 %all-to-all-done.2.x_ref = bf16[8,88,2048]{2,1,0:T(8,128)(2,1)S(1)} async-done(((bf16[8,88,2048]{2,1,0:T(8,128)(2,1)}), bf16[8,88,2048]{2,1,0:T(8,128)(2,1)S(1)}, u32[]{:S(2)}, u32[]{:S(2)}) %all-to-all-start.2) | async-done | bytes 2883616 | tf_op jit(solution)/shard_map/all_to_all | solution.py:327
  149.7 0.0 reduce-scatter.2.cloned.1.call-done
  149.7 0.0 copy-done.5
  149.7 0.0 copy-start.7
  149.7 0.9 copy-done.7
  150.6 1.3 finish.1
  (2 shorter events, 0.0 us)
Async XLA Ops:
  10.4 3.8 %copy-start.6 = (bf16[96,1152]{1,0:T(8,128)(2,1)S(1)}, bf16[96,1152]{1,0:T(8,128)(2,1)}, u32[]{:S(2)}) copy-start(bf16[96,1152]{1,0:T(8,128)(2,1)} %get-tuple-element.17.refs_0_) | copy-start | bytes 663556
  10.4 39.8 %all-to-all-start = ((bf16[8,88,2048]{2,1,0:T(8,128)(2,1)}), bf16[8,88,2048]{2,1,0:T(8,128)(2,1)S(1)}, u32[]{:S(2)}, u32[]{:S(2)}) async-start(bf16[8,88,2048]{2,1,0:T(8,128)(2,1)} %get-tuple-element.18), calls=%async_computation | async-start | bytes 5767168 | tf_op jit(solution)/shard_map/all_to_all | solution.py:287
  14.1 135.5 %reduce-scatter.2.cloned.1.call-start = ((), (), s32[]{:S(2)}) async-start(), calls=%async_computation.4 | async-start | bytes 1622016 | tf_op jit(solution)/shard_map/reduce_scatter | solution.py:326
  14.2 10.3 %collective-permute-start.4 = (bf16[96,1152]{1,0:T(8,128)(2,1)S(1)}, bf16[96,1152]{1,0:T(8,128)(2,1)S(1)}, u32[]{:S(2)}, u32[]{:S(2)}) collective-permute-start(bf16[96,1152]{1,0:T(8,128)(2,1)S(1)} %copy-done.6), channel_id=1, source_target_pairs={{0,56},{8,0},{16,8},{24,16},{32,24},{40,32},{48,40},{56,48},{1,57}... | collective-permute-start | bytes 663560 | tf_op jit(solution)/shard_map/ppermute | solution.py:31
  20.1 8.1 %collective-permute-start = (bf16[96,1152]{1,0:T(8,128)(2,1)S(1)}, bf16[96,1152]{1,0:T(8,128)(2,1)S(1)}, u32[]{:S(2)}, u32[]{:S(2)}) collective-permute-start(bf16[96,1152]{1,0:T(8,128)(2,1)S(1)} %copy-done.6), channel_id=1, source_target_pairs={{0,8},{8,16},{16,24},{24,32},{32,40},{40,48},{48,56},{56,0},{1,9},... | collective-permute-start | bytes 663560 | tf_op jit(solution)/shard_map/ppermute | solution.py:31
  24.5 7.2 %collective-permute-start.5 = (bf16[96,1152]{1,0:T(8,128)(2,1)S(1)}, bf16[96,1152]{1,0:T(8,128)(2,1)S(1)}, u32[]{:S(2)}, u32[]{:S(2)}) collective-permute-start(bf16[96,1152]{1,0:T(8,128)(2,1)S(1)} %collective-permute-done.4.refs_8_), channel_id=1, source_target_pairs={{0,56},{8,0},{16,8},{24,16},{32,24},{40,32},{48,40},{56,48},{1,57}... | collective-permute-start | bytes 663560 | tf_op jit(solution)/shard_map/ppermute | solution.py:31
  28.2 7.2 %collective-permute-start.1 = (bf16[96,1152]{1,0:T(8,128)(2,1)S(1)}, bf16[96,1152]{1,0:T(8,128)(2,1)S(1)}, u32[]{:S(2)}, u32[]{:S(2)}) collective-permute-start(bf16[96,1152]{1,0:T(8,128)(2,1)S(1)} %collective-permute-done.refs_1_), channel_id=1, source_target_pairs={{0,8},{8,16},{16,24},{24,32},{32,40},{40,48},{48,56},{56,0},{1,9},... | collective-permute-start | bytes 663560 | tf_op jit(solution)/shard_map/ppermute | solution.py:31
  31.7 7.1 %collective-permute-start.6 = (bf16[96,1152]{1,0:T(8,128)(2,1)S(1)}, bf16[96,1152]{1,0:T(8,128)(2,1)S(1)}, u32[]{:S(2)}, u32[]{:S(2)}) collective-permute-start(bf16[96,1152]{1,0:T(8,128)(2,1)S(1)} %collective-permute-done.5.refs_7_), channel_id=1, source_target_pairs={{0,56},{8,0},{16,8},{24,16},{32,24},{40,32},{48,40},{56,48},{1,57}... | collective-permute-start | bytes 663560 | tf_op jit(solution)/shard_map/ppermute | solution.py:31
  35.4 7.2 %collective-permute-start.2 = (bf16[96,1152]{1,0:T(8,128)(2,1)S(1)}, bf16[96,1152]{1,0:T(8,128)(2,1)S(1)}, u32[]{:S(2)}, u32[]{:S(2)}) collective-permute-start(bf16[96,1152]{1,0:T(8,128)(2,1)S(1)} %collective-permute-done.1.refs_2_), channel_id=1, source_target_pairs={{0,8},{8,16},{16,24},{24,32},{32,40},{40,48},{48,56},{56,0},{1,9},... | collective-permute-start | bytes 663560 | tf_op jit(solution)/shard_map/ppermute | solution.py:31
  38.9 6.1 %collective-permute-start.7 = (bf16[48,1152]{1,0:T(8,128)(2,1)S(1)}, bf16[48,1152]{1,0:T(8,128)(2,1)S(1)}, u32[]{:S(2)}, u32[]{:S(2)}) collective-permute-start(bf16[48,1152]{1,0:T(8,128)(2,1)S(1)} %slice.21), channel_id=1, source_target_pairs={{0,56},{8,0},{16,8},{24,16},{32,24},{40,32},{48,40},{56,48},{1,57}... | collective-permute-start | bytes 331784 | tf_op jit(solution)/shard_map/ppermute | solution.py:31
  42.7 6.0 %collective-permute-start.3 = (bf16[48,1152]{1,0:T(8,128)(2,1)S(1)}, bf16[48,1152]{1,0:T(8,128)(2,1)S(1)}, u32[]{:S(2)}, u32[]{:S(2)}) collective-permute-start(bf16[48,1152]{1,0:T(8,128)(2,1)S(1)} %slice.20), channel_id=1, source_target_pairs={{0,8},{8,16},{16,24},{24,32},{32,40},{40,48},{48,56},{56,0},{1,9},... | collective-permute-start | bytes 331784 | tf_op jit(solution)/shard_map/ppermute | solution.py:31
  48.9 1.3 copy-start
  50.1 1.5 copy-start.1
  54.3 3.0 %collective-permute-start.8 = (f32[2,176,768]{2,1,0:T(8,128)S(1)}, f32[2,176,768]{2,1,0:T(8,128)S(1)}, u32[]{:S(2)}, u32[]{:S(2)}) collective-permute-start(f32[2,176,768]{2,1,0:T(8,128)S(1)} %scores_give.1), channel_id=1, source_target_pairs={{0,1},{1,0},{2,3},{3,2},{4,5},{5,4},{6,7},{7,6},{8,9},{9,8},{10,11... | collective-permute-start | bytes 3244040 | tf_op jit(solution)/shard_map/ppermute | solution.py:31
  57.3 43.5 %copy-start.2 = (bf16[768,1152]{1,0:T(8,128)(2,1)S(1)}, bf16[768,1152]{1,0:T(8,128)(2,1)}, u32[]{:S(2)}) copy-start(bf16[768,1152]{1,0:T(8,128)(2,1)} %copy-done) | copy-start | bytes 5308420
  57.3 16.3 %collective-permute-start.9 = (f32[1,176,768]{2,1,0:T(8,128)S(1)}, f32[1,176,768]{2,1,0:T(8,128)S(1)}, u32[]{:S(2)}, u32[]{:S(2)}) collective-permute-start(f32[1,176,768]{2,1,0:T(8,128)S(1)} %slice_add_fusion), channel_id=1, source_target_pairs={{0,2},{2,0},{1,3},{3,1},{4,6},{6,4},{5,7},{7,5},{8,10},{10,8},{9,1... | collective-permute-start | bytes 1622024 | tf_op jit(solution)/shard_map/ppermute | solution.py:31
  90.0 8.8 %collective-permute-start.10 = (bf16[192,768]{1,0:T(8,128)(2,1)S(1)}, bf16[192,768]{1,0:T(8,128)(2,1)S(1)}, u32[]{:S(2)}, u32[]{:S(2)}) collective-permute-start(bf16[192,768]{1,0:T(8,128)(2,1)S(1)} %settle.1.e0_ref), channel_id=1, source_target_pairs={{0,2},{2,0},{1,3},{3,1},{4,6},{6,4},{5,7},{7,5},{8,10},{10,8},{9,1... | collective-permute-start | bytes 884744 | tf_op jit(solution)/shard_map/ppermute | solution.py:31
  98.8 1.6 collective-permute-start.11
  98.8 2.0 %collective-permute-start.12 = (bf16[192,768]{1,0:T(8,128)(2,1)S(1)}, bf16[192,768]{1,0:T(8,128)(2,1)S(1)}, u32[]{:S(2)}, u32[]{:S(2)}) collective-permute-start(bf16[192,768]{1,0:T(8,128)(2,1)S(1)} %collective-permute-done.10.e2_ref), channel_id=1, source_target_pairs={{0,1},{1,0},{2,3},{3,2},{4,5},{5,4},{6,7},{7,6},{8,9},{9,8},{10,11... | collective-permute-start | bytes 884744 | tf_op jit(solution)/shard_map/ppermute | solution.py:31
  107.2 1.6 copy-start.3
  108.8 1.1 copy-start.4
  109.9 39.7 %copy-start.5 = (bf16[88,1024]{1,0:T(8,128)(2,1)S(1)}, bf16[88,1024]{1,0:T(8,128)(2,1)}, u32[]{:S(2)}) copy-start(bf16[88,1024]{1,0:T(8,128)(2,1)} %p_ref.3) | copy-start | bytes 540676
  110.0 39.7 %all-to-all-start.2 = ((bf16[8,88,2048]{2,1,0:T(8,128)(2,1)}), bf16[8,88,2048]{2,1,0:T(8,128)(2,1)S(1)}, u32[]{:S(2)}, u32[]{:S(2)}) async-start(bf16[8,88,2048]{2,1,0:T(8,128)(2,1)} %bitcast.10), calls=%async_computation.3 | async-start | bytes 5767168 | tf_op jit(solution)/shard_map/all_to_all | solution.py:327
  149.7 0.9 copy-start.7
Sparse Core Ops, SparseCore 0:
  110.1 34.4 reduce-scatter.1
